TPU v7x, 256 devices: a whole 4x4x8 slice. The times are simulated.
256 devices in a mesh: seq: 64 (over z, x, core), tp: 4 (over y).
Axes of the slice: x: 4, y: 4, z: 8, core: 2. Of those that a mesh axis runs over, the one named last changes fastest.
Arguments:
- tokens: bfloat16 [32768, 4096], P('seq', 'tp'), may hold values from -6 to 6
- log_decay: float32 [32768, 16], P('seq', 'tp'), may hold values from -2 to 0
- w_query: bfloat16 [4096, 2048], P(None, 'tp'), may hold values from -0.09375 to 0.09375
- w_key: bfloat16 [4096, 512], P(None, 'tp'), may hold values from -0.09375 to 0.09375
- w_value: bfloat16 [4096, 512], P(None, 'tp'), may hold values from -0.09375 to 0.09375
- w_level: bfloat16 [4096, 144], P(None, 'tp'), may hold values from -0.09375 to 0.09375
- w_out: bfloat16 [2048, 4096], P('tp'), may hold values from -0.125 to 0.125
Outputs:
- mixed: bfloat16 [32768, 4096], P('seq', 'tp')
All inputs are finite; a program needn't handle non-finite values.
Results may differ from a plain program's by a relative error of at most 0.02.
Values may be sent and summed in bfloat16 or wider, within the bound.
A program may use at most 128 MiB of HBM per device.

v0:
```python
import jax
import jax.numpy as jnp
from jax import lax
from jax.sharding import PartitionSpec as P

BLOCK = 128


HIGHEST = lax.Precision.HIGHEST


def prefix(part, axis, combine, identity):
    place = lax.axis_index(axis)
    gathered = lax.all_gather(part, axis)
    state = jnp.zeros_like(part) + jnp.asarray(identity, part.dtype)

    def one(step, state):
        return combine(state, lax.dynamic_index_in_dim(gathered, step, 0, False))

    return lax.fori_loop(0, place, one, state)


def top_bit(differ, bit_count):
    result = jnp.zeros_like(differ)
    for shift in range(1, bit_count):
        result = result + (jnp.right_shift(differ, shift) > 0).astype(jnp.int32)
    return result


def split_pair(wide):
    upper_part = wide.astype(jnp.bfloat16)
    lower_part = (wide - upper_part.astype(jnp.float32)).astype(jnp.bfloat16)
    return (upper_part, lower_part)


def body(tokens, log_decay, w_query, w_key, w_value, w_level, w_out):
    rows = tokens.shape[0]
    heads_local = log_decay.shape[1]
    head_size = w_out.shape[0] // heads_local
    level_count = w_level.shape[1] // heads_local
    kv_local = w_key.shape[1] // head_size
    group_size = heads_local // kv_local
    matrices = (w_query, w_key, w_value, w_level)
    piece = lax.all_gather(tokens, "tp", axis=1, tiled=True)
    sums = tuple(
        (jnp.dot(piece, matrix, preferred_element_type=jnp.float32) for matrix in matrices)
    )
    query = sums[0].astype(jnp.bfloat16).reshape(rows, kv_local, group_size, head_size)
    keys_here = sums[1].astype(jnp.bfloat16).reshape(rows, kv_local, head_size)
    values_here = sums[2].astype(jnp.bfloat16).reshape(rows, kv_local, head_size)
    level_weight = jax.nn.softplus(sums[3]).reshape(rows, heads_local, level_count)
    decay_sum = jnp.cumsum(log_decay, axis=0)
    slab_total = decay_sum[rows - 1]
    before = prefix(slab_total, "seq", jnp.add, jnp.zeros_like(slab_total))
    ends_here = before + slab_total
    positions = jnp.arange(rows, dtype=jnp.int32)
    block_of = positions // BLOCK
    local_bits = (rows // BLOCK).bit_length() - 1
    block_differ = jnp.bitwise_xor(block_of[:, None], block_of[None, :])
    level_table = jnp.where(block_differ == 0, 0, 1 + top_bit(block_differ, local_bits))
    causal = positions[:, None] >= positions[None, :]
    decay_heads = decay_sum.T
    gaps = jnp.where(causal[None], decay_heads[:, :, None] - decay_heads[:, None, :], -jnp.inf)
    picked = jnp.zeros((heads_local, rows, rows), jnp.float32)
    for level in range(local_bits + 1):
        picked = picked + jnp.where(
            level_table[None] == level, level_weight[:, :, level].T[:, :, None], 0.0
        )
    scores = jnp.einsum(
        "tgqd,sgd->gqts", query, keys_here, preferred_element_type=jnp.float32
    ).reshape(heads_local, rows, rows)
    mixing = (picked * jnp.exp(gaps) * scores).reshape(kv_local, group_size, rows, rows)
    mixing_upper, mixing_lower = split_pair(mixing)
    local_part = jnp.einsum(
        "gqts,sgd->gqtd", mixing_upper, values_here, preferred_element_type=jnp.float32
    )
    local_part = local_part + jnp.einsum(
        "gqts,sgd->gqtd", mixing_lower, values_here, preferred_element_type=jnp.float32
    )
    local_part = local_part.reshape(heads_local, rows, head_size)
    keep_factor = jnp.exp(slab_total[None, :] - decay_sum).reshape(rows, kv_local, group_size)
    weighted_keys = keep_factor[:, :, :, None] * keys_here.astype(jnp.float32)[:, :, None, :]
    keys_upper, keys_lower = split_pair(weighted_keys)
    own_state = jnp.einsum(
        "tgqd,tge->gqde", keys_upper, values_here, preferred_element_type=jnp.float32
    )
    own_state = own_state + jnp.einsum(
        "tgqd,tge->gqde", keys_lower, values_here, preferred_element_type=jnp.float32
    )
    own_state = own_state.reshape(heads_local, head_size, head_size)
    seq_bits = lax.axis_size("seq").bit_length() - 1
    device = lax.axis_index("seq")
    empty = jnp.zeros((seq_bits, heads_local, head_size, head_size), jnp.float32)
    states = lax.all_gather(own_state[None], "seq", axis=0, tiled=True)
    slab_ends = lax.all_gather(ends_here[None], "seq", axis=0, tiled=True)
    sources = jnp.arange(states.shape[0], dtype=jnp.int32)
    earlier = sources < device
    highest_bit = top_bit(jnp.bitwise_xor(sources, device), seq_bits)
    onehot = jnp.logical_and(
        highest_bit[:, None] == jnp.arange(seq_bits, dtype=jnp.int32)[None, :], earlier[:, None]
    ).astype(jnp.float32)
    fading = jnp.exp(jnp.where(earlier[:, None], before[None, :] - slab_ends, -jnp.inf))
    buckets = empty + jnp.einsum("nb,nh,nhde->bhde", onehot, fading, states, precision=HIGHEST)
    query_heads = query.reshape(rows, heads_local, head_size)
    buckets_upper, buckets_lower = split_pair(buckets)
    per_level = jnp.einsum(
        "thd,bhde->bthe", query_heads, buckets_upper, preferred_element_type=jnp.float32
    )
    per_level = per_level + jnp.einsum(
        "thd,bhde->bthe", query_heads, buckets_lower, preferred_element_type=jnp.float32
    )
    span_weight = (
        level_weight[:, :, local_bits + 1 : local_bits + 1 + seq_bits]
        * jnp.exp(decay_sum)[:, :, None]
    )
    remote_part = jnp.einsum("bthe,thb->hte", per_level, span_weight, precision=HIGHEST)
    combined = local_part + remote_part
    normed = (
        combined * lax.rsqrt(jnp.mean(combined * combined, axis=-1, keepdims=True) + 1e-05)
    ).astype(jnp.bfloat16)
    partial_out = jnp.einsum(
        "htd,hde->te",
        normed,
        w_out.reshape(heads_local, head_size, w_out.shape[1]),
        preferred_element_type=jnp.float32,
    )
    return lax.psum_scatter(partial_out.astype(jnp.bfloat16), "tp", scatter_dimension=1, tiled=True)


def solution(mesh):
    in_specs = (
        P("seq", "tp"),
        P("seq", "tp"),
        P(None, "tp"),
        P(None, "tp"),
        P(None, "tp"),
        P(None, "tp"),
        P("tp", None),
    )
    out_specs = P("seq", "tp")
    return jax.shard_map(body, mesh=mesh, in_specs=in_specs, out_specs=out_specs, check_vma=False)
```

profile of v0, /device:TPU:1, one launch (start us, length us, event | category | flops | bytes accessed | tf_op | source)
XLA Modules:
  0.0 341.4 jit_solution(4485512293242226166)
XLA Ops:
  6.5 0.0 copy-start
  6.5 0.0 all-gather.6.cloned.1.call-start
  6.5 0.7 all-gather.6.cloned.1.call-update
  7.3 0.0 all-gather.8.cloned.1.call-start
  7.3 0.7 reshape.296
  8.0 1.2 reduce-window.6
  9.2 0.2 slice_reduce_fusion
  9.4 0.2 reduce-window.9
  9.6 0.1 add_bitcast_fusion
  9.6 0.2 slice_reduce_fusion.1
  9.8 0.1 bitcast_exponential_fusion
  9.9 53.9 %all-gather.6.cloned.1.call-done = bf16[512,4096]{1,0:T(8,128)(2,1)} async-done(((bf16[512,1024]{1,0:T(8,128)(2,1)}), bf16[512,4096]{1,0:T(8,128)(2,1)}) %all-gather.6.cloned.1.call-update) | async-done | bytes 4194320 | tf_op jit(solution)/shard_map/all_gather | solution.py:44
  63.8 0.0 copy-done
  63.8 3.4 %convolution_convert_fusion.2 = bf16[512,128]{1,0:T(8,128)(2,1)S(1)} fusion(bf16[512,4096]{1,0:T(8,128)(2,1)} %all-gather.6.cloned.1.call-done, bf16[4096,128]{1,0:T(8,128)(2,1)S(1)} %copy-done), kind=kOutput, calls=%fused_computation.24 | convolution fusion | flops 536936448 | bytes 5373952 | tf_op jit(solution)/shard_map/dot_general | solution.py:46
  67.3 0.0 copy-start.6
  67.3 0.1 copy.68
  67.4 0.0 copy-start.4
  67.4 3.8 %fusion.14 = bf16[512,128,1]{1,0,2:T(8,128)(2,1)S(1)} fusion(bf16[512,4096]{1,0:T(8,128)(2,1)} %all-gather.6.cloned.1.call-done, bf16[4096,128]{1,0:T(8,128)(2,1)} %param.13), kind=kOutput, calls=%fused_computation.25 | convolution fusion | flops 536936448 | bytes 5373952 | tf_op jit(solution)/shard_map/dot_general | solution.py:46
  71.2 0.3 fusion.25
  71.5 1.0 convolution_add_fusion
  72.5 0.0 all-gather.8.cloned.1.call-update
  72.5 0.0 reduce-scatter.2.cloned.1.call-start
  72.6 0.0 copy-done.6
  72.6 0.7 dynamic-slice
  73.9 41.7 %all-gather.2 = f32[64,1,4]{2,1,0:T(1,128)S(1)} all-gather(f32[1,1,4]{2,1,0:T(1,128)S(1)} %bitcast.109), channel_id=1, replica_groups=mesh['seq'=64,'tp'=4] {'seq'}, dimensions={0}, use_global_device_ids=true | all-gather | bytes 1040 | tf_op jit(solution)/shard_map/all_gather | solution.py:14
  115.7 0.1 add_dynamic-update-slice_fusion
  115.8 124.5 %all-reduce = f32[256]{0:T(256)S(1)} all-reduce(f32[256]{0:T(256)S(1)} %add_dynamic-update-slice_fusion), channel_id=2, replica_groups=mesh['seq'=64,'tp'=4] {'seq'}, use_global_device_ids=true, to_apply=%add | all-reduce | flops 256 | bytes 2048
  240.2 0.1 reshape.302
  240.4 0.1 copy.67
  240.5 0.8 iota_compare_fusion
  241.2 0.1 select_exponential_fusion
  241.3 0.7 fusion.21
  242.0 0.0 copy-done.4
  242.0 3.6 %compare_select_fusion = f32[512,36]{0,1:T(8,128)S(1)} fusion(bf16[512,4096]{1,0:T(8,128)(2,1)} %all-gather.6.cloned.1.call-done, bf16[4096,36]{0,1:T(8,128)(2,1)S(1)} %copy-done.4), kind=kOutput, calls=%fused_computation.46 | convolution fusion | flops 151105536 | bytes 4562944 | tf_op jit(solution)/shard_map/dot_general | solution.py:46
  245.7 0.0 copy-start.5
  245.8 5.9 %convolution_convert_fusion = bf16[512,512]{0,1:T(8,128)(2,1)S(1)} fusion(bf16[512,4096]{1,0:T(8,128)(2,1)} %all-gather.6.cloned.1.call-done, bf16[4096,512]{1,0:T(8,128)(2,1)} %param.11), kind=kOutput, calls=%fused_computation.20 | convolution fusion | flops 2147745792 | bytes 8912896 | tf_op jit(solution)/shard_map/dot_general | solution.py:46
  251.6 0.0 copy-done.5
  251.6 2.6 bitcast_multiply_fusion.1
  254.2 0.0 copy-start.1
  254.2 1.9 copy-done.1
  256.2 0.7 fusion.4
  256.9 0.0 all-gather.8.cloned.1.call-done
  256.9 20.4 %fusion = f32[6,4,128,128]{3,0,2,1:T(8,128)S(1)} fusion(f32[64,4,128,128]{3,2,1,0:T(8,128)} %bitcast.101, f32[64,4]{0,1:T(4,128)S(1)} %select_exponential_fusion, s32[64]{0:T(128)S(1)} %fusion.45, pred[64]{0:T(512)(128)(4,1)S(1)} %iota_compare_fusion.2), kind=kOutput, calls=%fused_computation.2 | convolution fusion | flops 306184960 | bytes 18351424 | tf_op jit(solution)/shard_map/nb,nh,nhde->bhde/dot_general | solution.py:103
  277.3 1.0 fusion.23
  278.3 0.0 copy-start.2
  278.3 1.2 fusion.2
  279.5 1.0 copy-done.2
  280.5 0.0 copy-start.3
  280.5 0.9 multiply_reduce_fusion
  281.4 1.3 copy-done.3
  282.7 4.4 %bitcast_convert_fusion = bf16[512,4096]{1,0:T(8,128)(2,1)} fusion(bf16[4,128,4096]{2,1,0:T(8,128)(2,1)S(1)} %bitcast.102, f32[4,512,128]{1,2,0:T(8,128)S(1)} %get-tuple-element.48, f32[4,512]{1,0:T(4,128)S(1)} %add_rsqrt_fusion), kind=kOutput, calls=%fused_computation.3 | convolution fusion | flops 2150105088 | bytes 9445376 | tf_op jit(solution)/shard_map/htd,hde->te/dot_general | solution.py:121
  287.1 0.0 reduce-scatter.2.cloned.1.call-update
  287.1 47.8 %reduce-scatter.2.cloned.1.call-done = bf16[512,1024]{1,0:T(8,128)(2,1)} async-done(((bf16[512,4096]{1,0:T(8,128)(2,1)}), bf16[512,1024]{1,0:T(8,128)(2,1)}) %reduce-scatter.2.cloned.1.call-update) | async-done | bytes 1048592 | tf_op jit(solution)/shard_map/reduce_scatter | solution.py:127
  (14 shorter events, 0.1 us)
Async XLA Ops:
  6.5 57.3 %copy-start = (bf16[4096,128]{1,0:T(8,128)(2,1)S(1)}, bf16[4096,128]{1,0:T(8,128)(2,1)}, u32[]{:S(2)}) copy-start(bf16[4096,128]{1,0:T(8,128)(2,1)} %param.12) | copy-start | bytes 3145732
  6.5 57.3 %all-gather.6.cloned.1.call-start = ((), (), s32[]{:S(2)}) async-start(), calls=%async_computation.1 | async-start | bytes 5242880 | tf_op jit(solution)/shard_map/all_gather | solution.py:44
  7.3 249.6 %all-gather.8.cloned.1.call-start = ((), (), s32[]{:S(2)}) async-start(), calls=%async_computation.3 | async-start | bytes 17039360 | tf_op jit(solution)/shard_map/all_gather | solution.py:94
  67.3 5.3 %copy-start.6 = (u32[256]{0:T(256)S(1)}, u32[256]{0:T(256)}, u32[]{:S(2)}) copy-start(u32[256]{0:T(256)} %constant.67) | copy-start | bytes 3076
  67.4 174.6 %copy-start.4 = (bf16[4096,36]{0,1:T(8,128)(2,1)S(1)}, bf16[4096,36]{0,1:T(8,128)(2,1)}, u32[]{:S(2)}) copy-start(bf16[4096,36]{0,1:T(8,128)(2,1)} %param.14) | copy-start | bytes 884740
  72.5 262.3 %reduce-scatter.2.cloned.1.call-start = ((), (), s32[]{:S(2)}) async-start(), calls=%async_computation.2 | async-start | bytes 5242880 | tf_op jit(solution)/shard_map/reduce_scatter | solution.py:127
  245.7 5.9 %copy-start.5 = (pred[512,512]{0,1:T(8,128)(4,1)S(1)}, pred[512,512]{0,1:T(8,128)(4,1)}, u32[]{:S(2)}) copy-start(pred[512,512]{0,1:T(8,128)(4,1)} %iota_compare_fusion) | copy-start | bytes 786436
  254.2 1.9 copy-start.1
  278.3 2.2 copy-start.2
  280.5 2.2 copy-start.3
Sparse Core Ops, SparseCore 0:
  9.2 54.6 all-gather.5
  72.7 100.9 all-gather.7
  287.2 47.6 reduce-scatter.1
where the time goes:
time: 342 us; the launch traced here: 341 us
  blocking collectives  166 us (49%)
  waiting for transfers between devices  102 us (30%)
  matrix products  49.1 us (14%)
  between operations  14 us (4%)
  local copies, waits for them, and re-layouts  6.27 us (2%)
    unnamed x1, blocking collectives  124 us
    all_gather x1, waiting for transfers between devices, body(): piece = lax.all_gather(tokens, 'tp', axis=1, tiled=True)  53.9 us
    reduce_scatter x1, waiting for transfers between devices, body(): lax.psum_scatter(partial_out.astype(jnp.bfloat16), 'tp', scatter_dimensio...  47.8 us
    all_gather x1, blocking collectives, prefix(): gathered = lax.all_gather(part, axis)  41.7 us
    dot_general x1, matrix products, body(): jnp.einsum('nb,nh,nhde->bhde', onehot, fading, states, precision=HIGHEST)  20.4 us
    dot_general x4, matrix products, body(): jnp.dot(piece, matrix, preferred_element_type=jnp.float32)  16.7 us
  transfers between devices with their start and end apart: 3, of which 2 were waited for; matrix products, arithmetic and copies ran while one was open for 5% of the time, Pallas kernels for 0%

commit v1 on v0

v1 whole, which is shorter than its diff:
```python
import jax
import jax.numpy as jnp
from jax import lax
from jax.sharding import PartitionSpec as P

BLOCK = 128
HIGHEST = lax.Precision.HIGHEST
F32 = jnp.float32
BF16 = jnp.bfloat16


def body(tokens, log_decay, w_query, w_key, w_value, w_level, w_out):
    rows = tokens.shape[0]
    heads = log_decay.shape[1]
    size = w_out.shape[0] // heads
    level_count = w_level.shape[1] // heads
    blocks = rows // BLOCK
    local_bits = blocks.bit_length() - 1
    seq_size = lax.axis_size("seq")
    seq_bits = seq_size.bit_length() - 1
    device = lax.axis_index("seq")

    positions = jnp.arange(rows, dtype=jnp.int32)
    triangle = (positions[:, None] >= positions[None, :]).astype(F32)
    decay = jnp.dot(triangle, log_decay, precision=HIGHEST)
    total = decay[rows - 1]

    def swap(x, bit):
        pairs = [(i, i ^ (1 << bit)) for i in range(seq_size)]
        return lax.ppermute(x, "seq", pairs)

    group, before = total, jnp.zeros_like(total)
    befores, fades = [], []
    for bit in range(seq_bits):
        upper = (jnp.right_shift(device, bit) & 1) == 1
        other = swap(group, bit)
        befores.append(jnp.where(upper, before, -jnp.inf))
        fades.append(jnp.exp(jnp.where(upper, group, other)))
        before = before + jnp.where(upper, other, 0.0)
        group = group + other

    piece = lax.all_gather(tokens, "tp", axis=1, tiled=True)
    dot = lambda a, b: jnp.dot(a, b, preferred_element_type=F32)
    keys = dot(piece, w_key).astype(BF16)
    values = dot(piece, w_value).astype(BF16)
    keep = jnp.exp(total[None, :] - decay)
    weighted = (keep.T[:, :, None] * keys.astype(F32)[None]).astype(BF16)
    state = jnp.einsum("htd,te->hde", weighted, values, preferred_element_type=F32)
    buckets = []
    for bit in range(seq_bits):
        upper = (jnp.right_shift(device, bit) & 1) == 1
        other = swap(state.astype(BF16), bit)
        buckets.append(other)
        wide = other.astype(F32)
        low = jnp.where(upper, wide, state)
        high = jnp.where(upper, state, wide)
        state = high + fades[bit][:, None, None] * low

    query = dot(piece, w_query).astype(BF16).reshape(rows, heads, size)
    level = jax.nn.softplus(dot(piece, w_level)).reshape(rows, heads, level_count)
    qb = query.reshape(blocks, BLOCK, heads, size)
    kb = keys.reshape(blocks, BLOCK, size)
    vb = values.reshape(blocks, BLOCK, size)
    lb = level.reshape(blocks, BLOCK, heads, level_count)
    db = decay.reshape(blocks, BLOCK, heads)
    scores = jnp.einsum("cihd,cjd->hcij", qb, kb, preferred_element_type=F32)
    inside = jnp.arange(BLOCK)
    causal = inside[:, None] >= inside[None, :]
    dh = db.transpose(2, 0, 1)
    gaps = jnp.where(causal, dh[:, :, :, None] - dh[:, :, None, :], -jnp.inf)
    mixing = lb[:, :, :, 0].transpose(2, 0, 1)[:, :, :, None] * jnp.exp(gaps) * scores
    out = jnp.einsum("hcij,cje->hcie", mixing.astype(BF16), vb, preferred_element_type=F32)
    ends = db[:, BLOCK - 1]
    weighted = jnp.exp(ends[:, None] - db).transpose(2, 0, 1)[..., None] * kb.astype(F32)[None]
    small = jnp.einsum("hcjd,cje->hcde", weighted.astype(BF16), vb, preferred_element_type=F32)
    small_ends = ends
    parts = [out[:, c] for c in range(blocks)]
    for bit in range(local_bits):
        for c in range(blocks):
            if (c >> bit) & 1:
                s = (c >> bit) - 1
                factor = lb[c, :, :, 1 + bit] * jnp.exp(db[c] - small_ends[s][None, :])
                got = jnp.einsum("ihd,hde->hie", qb[c], small[:, s].astype(BF16), preferred_element_type=F32)
                parts[c] = parts[c] + factor.T[:, :, None] * got
        fade = jnp.exp(small_ends[1::2] - small_ends[0::2])
        small = small[:, 1::2] + fade.T[:, :, None, None] * small[:, 0::2]
        small_ends = small_ends[1::2]
    combined = jnp.concatenate(parts, axis=1)
    for bit in range(seq_bits):
        factor = level[:, :, 1 + local_bits + bit] * jnp.exp(decay + befores[bit][None, :])
        got = jnp.einsum("thd,hde->hte", query, buckets[bit], preferred_element_type=F32)
        combined = combined + factor.T[:, :, None] * got
    normed = (
        combined * lax.rsqrt(jnp.mean(combined * combined, axis=-1, keepdims=True) + 1e-05)
    ).astype(BF16)
    wide = normed.transpose(1, 0, 2).reshape(rows, heads * size)
    partial = dot(wide, w_out)
    return lax.psum_scatter(partial.astype(BF16), "tp", scatter_dimension=1, tiled=True)


def solution(mesh):
    in_specs = (
        P("seq", "tp"),
        P("seq", "tp"),
        P(None, "tp"),
        P(None, "tp"),
        P(None, "tp"),
        P(None, "tp"),
        P("tp", None),
    )
    return jax.shard_map(
        body, mesh=mesh, in_specs=in_specs, out_specs=P("seq", "tp"), check_vma=False
    )
```

time: 342 us -> 198 us (0.58)
  blocking collectives: 166 us -> 0 us
  starting transfers between devices: 0.08 us -> 19.8 us
  matrix products: 49.1 us -> 36.4 us
  waiting for transfers between devices: 102 us -> 111 us
  other arithmetic: 3.27 us -> 7.64 us
    unnamed x1 -> x0, blocking collectives: 124 us -> none
    all_gather x1 -> x0, blocking collectives: 41.7 us -> none  [prefix(): gathered = lax.all_gather(part, axis)]
    ppermute x0 -> x11, waiting for transfers between devices: none -> 22.4 us  [swap(): return lax.ppermute(x, 'seq', pairs)]
    all_gather x1, waiting for transfers between devices: 53.9 us -> 33.4 us  [body(): piece = lax.all_gather(tokens, 'tp', axis=1, tiled=True)]
    ppermute x0 -> x11, starting transfers between devices: none -> 19.8 us  [swap(): return lax.ppermute(x, 'seq', pairs)]
    dot_general x13 -> x19, matrix products: 49.1 us -> 36.4 us  [the longest x5 23.2 us: body(): dot = lambda a, b: jnp.dot(a, b, preferred_element_type=F32)]
    reduce_scatter x1, waiting for transfers between devices: 47.8 us -> 54.5 us  [body(): lax.psum_scatter(partial.astype(BF16), 'tp', scatter_dimension=1, tiled=T...]
  transfers between devices with their start and end apart: 3 -> 13, of which waited for: 2 -> 11; matrix products, arithmetic and copies ran while one was open for 5% -> 9% of each run, Pallas kernels for 0% -> 0%
where the time goes in v1:
time: 198 us; the launch traced here: 197 us
  waiting for transfers between devices  111 us (56%)
  matrix products  36.4 us (18%)
  starting transfers between devices  19.8 us (10%)
  between operations  13.9 us (7%)
  local copies, waits for them, and re-layouts  8.63 us (4%)
  other arithmetic  7.64 us (4%)
    reduce_scatter x1, waiting for transfers between devices, body(): lax.psum_scatter(partial.astype(BF16), 'tp', scatter_dimension=1, tiled=T...  54.5 us
    all_gather x1, waiting for transfers between devices, body(): piece = lax.all_gather(tokens, 'tp', axis=1, tiled=True)  33.4 us
    dot_general x5, matrix products, body(): dot = lambda a, b: jnp.dot(a, b, preferred_element_type=F32)  23.2 us
    ppermute x11, waiting for transfers between devices, swap(): return lax.ppermute(x, 'seq', pairs)  22.4 us
    ppermute x11, starting transfers between devices, swap(): return lax.ppermute(x, 'seq', pairs)  19.8 us
    dot_general x4, matrix products, body(): jnp.einsum('ihd,hde->hie', qb[c], small[:, s].astype(BF16), preferred_ele...  3.96 us
  transfers between devices with their start and end apart: 13, of which 11 were waited for; matrix products, arithmetic and copies ran while one was open for 9% of the time, Pallas kernels for 0%

profile of v1, /device:TPU:1, one launch (start us, length us, event | category | flops | bytes accessed | tf_op | source)
XLA Modules:
  0.0 197.4 jit_solution(4253804932975548665)
XLA Ops:
  6.5 0.7 all-gather.2.cloned.1.call-update
  7.3 1.1 fusion.16
  8.4 0.3 slice_reduce_fusion
  8.7 3.3 %collective-permute-start.1 = (f32[4]{0:T(128)S(1)}, f32[4]{0:T(128)S(1)}, u32[]{:S(2)}, u32[]{:S(2)}) collective-permute-start(f32[4]{0:T(128)S(1)} %slice_reduce_fusion), channel_id=1, source_target_pairs={{0,4},{4,0},{8,12},{12,8},{16,20},{20,16},{24,28},{28,24},{32,36},... | collective-permute-start | bytes 56 | tf_op jit(solution)/shard_map/ppermute | solution.py:30
  12.4 0.7 copy.134
  13.1 0.6 copy.138
  13.7 0.6 copy.55
  14.4 0.6 iota_compare_fusion.2
  15.0 0.5 slice_bitcast_fusion.9
  15.6 0.6 fusion.66
  16.2 2.4 %collective-permute-done.3 = f32[4]{0:T(128)S(1)} collective-permute-done((f32[4]{0:T(128)S(1)}, f32[4]{0:T(128)S(1)}, u32[]{:S(2)}, u32[]{:S(2)}) %collective-permute-start.3) | collective-permute-done | bytes 48 | tf_op jit(solution)/shard_map/ppermute | solution.py:30
  18.6 0.6 broadcast_select_fusion.9
  19.2 1.0 collective-permute-start.5
  20.2 2.9 %collective-permute-done.5 = f32[4]{0:T(128)S(1)} collective-permute-done((f32[4]{0:T(128)S(1)}, f32[4]{0:T(128)S(1)}, u32[]{:S(2)}, u32[]{:S(2)}) %collective-permute-start.5) | collective-permute-done | bytes 48 | tf_op jit(solution)/shard_map/ppermute | solution.py:30
  23.1 0.5 fusion.85
  23.6 2.4 %collective-permute-done.7 = f32[4]{0:T(128)S(1)} collective-permute-done((f32[4]{0:T(128)S(1)}, f32[4]{0:T(128)S(1)}, u32[]{:S(2)}, u32[]{:S(2)}) %collective-permute-start.7) | collective-permute-done | bytes 48 | tf_op jit(solution)/shard_map/ppermute | solution.py:30
  26.0 0.6 fusion.84
  26.6 1.4 collective-permute-start.9
  28.0 1.9 collective-permute-done.9
  29.9 0.6 broadcast_select_fusion.3
  30.5 33.4 %all-gather.2.cloned.1.call-done = bf16[512,4096]{1,0:T(8,128)(2,1)} async-done(((bf16[512,1024]{1,0:T(8,128)(2,1)}), bf16[512,4096]{1,0:T(8,128)(2,1)}) %all-gather.2.cloned.1.call-update) | async-done | bytes 4194320 | tf_op jit(solution)/shard_map/all_gather | solution.py:42
  63.9 3.6 %compare_select_fusion = f32[512,36]{0,1:T(8,128)S(1)} fusion(bf16[512,4096]{1,0:T(8,128)(2,1)} %all-gather.2.cloned.1.call-done, bf16[4096,36]{0,1:T(8,128)(2,1)} %param.12), kind=kOutput, calls=%fused_computation.79 | convolution fusion | flops 151105536 | bytes 4562944 | tf_op jit(solution)/shard_map/dot_general | solution.py:43
  67.6 0.6 fusion.82
  68.2 5.8 %convolution_convert_fusion.1 = bf16[512,512]{0,1:T(8,128)(2,1)S(1)} fusion(bf16[512,4096]{1,0:T(8,128)(2,1)} %all-gather.2.cloned.1.call-done, bf16[4096,512]{1,0:T(8,128)(2,1)} %param.9), kind=kOutput, calls=%fused_computation.17 | convolution fusion | flops 2147745792 | bytes 8912896 | tf_op jit(solution)/shard_map/dot_general | solution.py:43
  74.1 0.8 fusion.80
  74.9 0.7 reshape.80
  75.6 0.6 copy.54
  76.2 3.4 %convolution_convert_fusion.2 = bf16[512,128]{1,0:T(8,128)(2,1)S(1)} fusion(bf16[512,4096]{1,0:T(8,128)(2,1)} %all-gather.2.cloned.1.call-done, bf16[4096,128]{1,0:T(8,128)(2,1)S(1)} %copy-done), kind=kOutput, calls=%fused_computation.27 | convolution fusion | flops 536936448 | bytes 5373952 | tf_op jit(solution)/shard_map/dot_general | solution.py:43
  79.8 3.7 %convolution_convert_fusion.3 = bf16[512,128]{1,0:T(8,128)(2,1)S(1)} fusion(bf16[512,4096]{1,0:T(8,128)(2,1)} %all-gather.2.cloned.1.call-done, bf16[4096,128]{1,0:T(8,128)(2,1)} %param.11), kind=kOutput, calls=%fused_computation.28 | convolution fusion | flops 536936448 | bytes 5373952 | tf_op jit(solution)/shard_map/dot_general | solution.py:43
  83.6 0.9 fusion.87
  84.6 1.2 fusion.81
  85.9 0.7 fusion.57
  86.6 1.0 fusion.86
  87.5 0.7 collective-permute-start
  88.4 2.8 %convolution_bitcast_fusion.1 = f32[4,4,128,128]{3,2,0,1:T(8,128)} fusion(bf16[4,128,128,1]{2,1,3,0:T(8,128)(2,1)} %bitcast.198, bf16[4,128,128,1]{2,1,3,0:T(8,128)(2,1)S(1)} %bitcast.194, bf16[4,128,4,128]{1,0,3,2:T(4,128)(2,1)S(1)} %reshape_reshape.7, f32[4,4,128]{2,0,1:T(4,128)} %copy.55, f32[4,4,128]{2,0,1:T(4,128)} %copy.54, ...), kind=kOutput, calls=%fused_computation.14 | convolution fusion | flops 135528448 | bytes 1867776 | tf_op jit(solution)/shard_map/hcij,cje->hcie/dot_general | solution.py:72
  91.2 0.8 fusion.63
  92.0 1.2 fusion.9
  93.2 0.2 fusion.8
  93.4 1.3 fusion.10
  94.7 1.3 fusion.11
  96.0 0.8 fusion.74
  96.8 1.3 collective-permute-start.2
  98.1 1.0 slice_bitcast_fusion.3
  99.0 3.0 %collective-permute-done.2 = bf16[4,128,128]{2,1,0:T(8,128)(2,1)S(1)} collective-permute-done((bf16[4,128,128]{2,1,0:T(8,128)(2,1)S(1)}, bf16[4,128,128]{2,1,0:T(8,128)(2,1)S(1)}, u32[]{:S(2)}, u32[]{:S(2)}) %collective-permute-start.2) | collective-permute-done | bytes 131104 | tf_op jit(solution)/shard_map/ppermute | solution.py:30
  102.0 0.8 fusion.43
  102.8 2.8 %collective-permute-start.4 = (bf16[4,128,128]{2,1,0:T(8,128)(2,1)S(1)}, bf16[4,128,128]{2,1,0:T(8,128)(2,1)S(1)}, u32[]{:S(2)}, u32[]{:S(2)}) collective-permute-start(bf16[4,128,128]{2,1,0:T(8,128)(2,1)S(1)} %fusion.43), channel_id=1, source_target_pairs={{0,16},{4,20},{8,24},{12,28},{16,0},{20,4},{24,8},{28,12},{32,48},... | collective-permute-start | bytes 393224 | tf_op jit(solution)/shard_map/ppermute | solution.py:30
  105.6 0.5 convolution_multiply_fusion.4
  106.1 2.5 %collective-permute-done.4 = bf16[4,128,128]{2,1,0:T(8,128)(2,1)S(1)} collective-permute-done((bf16[4,128,128]{2,1,0:T(8,128)(2,1)S(1)}, bf16[4,128,128]{2,1,0:T(8,128)(2,1)S(1)}, u32[]{:S(2)}, u32[]{:S(2)}) %collective-permute-start.4) | collective-permute-done | bytes 131104 | tf_op jit(solution)/shard_map/ppermute | solution.py:30
  108.7 0.2 fusion.77
  108.9 1.4 collective-permute-start.6
  110.3 0.5 convolution_multiply_fusion.3
  110.8 2.0 %collective-permute-done.6 = bf16[4,128,128]{2,1,0:T(8,128)(2,1)S(1)} collective-permute-done((bf16[4,128,128]{2,1,0:T(8,128)(2,1)S(1)}, bf16[4,128,128]{2,1,0:T(8,128)(2,1)S(1)}, u32[]{:S(2)}, u32[]{:S(2)}) %collective-permute-start.6) | collective-permute-done | bytes 131104 | tf_op jit(solution)/shard_map/ppermute | solution.py:30
  112.9 2.3 %collective-permute-start.8 = (bf16[4,128,128]{2,1,0:T(8,128)(2,1)S(1)}, bf16[4,128,128]{2,1,0:T(8,128)(2,1)S(1)}, u32[]{:S(2)}, u32[]{:S(2)}) collective-permute-start(bf16[4,128,128]{2,1,0:T(8,128)(2,1)S(1)} %fusion.42), channel_id=1, source_target_pairs={{0,64},{4,68},{8,72},{12,76},{16,80},{20,84},{24,88},{28,92},{32,9... | collective-permute-start | bytes 393224 | tf_op jit(solution)/shard_map/ppermute | solution.py:30
  115.3 0.5 convolution_multiply_fusion.2
  115.8 3.4 %collective-permute-done.8 = bf16[4,128,128]{2,1,0:T(8,128)(2,1)S(1)} collective-permute-done((bf16[4,128,128]{2,1,0:T(8,128)(2,1)S(1)}, bf16[4,128,128]{2,1,0:T(8,128)(2,1)S(1)}, u32[]{:S(2)}, u32[]{:S(2)}) %collective-permute-start.8) | collective-permute-done | bytes 131104 | tf_op jit(solution)/shard_map/ppermute | solution.py:30
  119.3 5.5 %collective-permute-start.10 = (bf16[4,128,128]{2,1,0:T(8,128)(2,1)S(1)}, bf16[4,128,128]{2,1,0:T(8,128)(2,1)S(1)}, u32[]{:S(2)}, u32[]{:S(2)}) collective-permute-start(bf16[4,128,128]{2,1,0:T(8,128)(2,1)S(1)} %fusion.39), channel_id=1, source_target_pairs={{0,128},{4,132},{8,136},{12,140},{16,144},{20,148},{24,152},{28,15... | collective-permute-start | bytes 393224 | tf_op jit(solution)/shard_map/ppermute | solution.py:30
  124.8 0.5 convolution_multiply_fusion.1
  125.3 2.0 collective-permute-done.10
  127.3 0.5 convolution_multiply_fusion
  127.8 1.1 multiply_reduce_fusion
  128.9 0.3 fusion.18
  129.3 0.2 copy.100
  129.5 6.5 %convolution_convert_fusion = bf16[512,4096]{1,0:T(8,128)(2,1)} fusion(bf16[512,512]{0,1:T(8,128)(2,1)S(1)} %bitcast.190, bf16[512,4096]{1,0:T(8,128)(2,1)} %param.13), kind=kOutput, calls=%fused_computation | convolution fusion | flops 2149580800 | bytes 8912896 | tf_op jit(solution)/shard_map/dot_general | solution.py:43
  136.0 54.5 %reduce-scatter.2.cloned.1.call-done = bf16[512,1024]{1,0:T(8,128)(2,1)} async-done(((bf16[512,4096]{1,0:T(8,128)(2,1)}), bf16[512,1024]{1,0:T(8,128)(2,1)}) %reduce-scatter.2.cloned.1.call-update) | async-done | bytes 1048592 | tf_op jit(solution)/shard_map/reduce_scatter | solution.py:98
  (69 shorter events, 1.4 us)
Async XLA Ops:
  6.5 69.7 %copy-start = (bf16[4096,128]{1,0:T(8,128)(2,1)S(1)}, bf16[4096,128]{1,0:T(8,128)(2,1)}, u32[]{:S(2)}) copy-start(bf16[4096,128]{1,0:T(8,128)(2,1)} %param.10) | copy-start | bytes 3145732
  6.5 57.3 %all-gather.2.cloned.1.call-start = ((), (), s32[]{:S(2)}) async-start(), calls=%async_computation.1 | async-start | bytes 5242880 | tf_op jit(solution)/shard_map/all_gather | solution.py:42
  7.3 183.3 %reduce-scatter.2.cloned.1.call-start = ((), (), s32[]{:S(2)}) async-start(), calls=%async_computation.2 | async-start | bytes 5242880 | tf_op jit(solution)/shard_map/reduce_scatter | solution.py:98
  8.6 55.2 %copy-start.9 = (f32[4]{0:T(128)}, f32[4]{0:T(128)S(1)}, u32[]{:S(2)}) copy-start(f32[4]{0:T(128)S(1)} %slice_reduce_fusion) | copy-start | bytes 52
  8.7 6.9 %collective-permute-start.1 = (f32[4]{0:T(128)S(1)}, f32[4]{0:T(128)S(1)}, u32[]{:S(2)}, u32[]{:S(2)}) collective-permute-start(f32[4]{0:T(128)S(1)} %slice_reduce_fusion), channel_id=1, source_target_pairs={{0,4},{4,0},{8,12},{12,8},{16,20},{20,16},{24,28},{28,24},{32,36},... | collective-permute-start | bytes 56 | tf_op jit(solution)/shard_map/ppermute | solution.py:30
  14.4 1.8 copy-start.19
  16.2 2.4 %collective-permute-start.3 = (f32[4]{0:T(128)S(1)}, f32[4]{0:T(128)S(1)}, u32[]{:S(2)}, u32[]{:S(2)}) collective-permute-start(f32[4]{0:T(128)S(1)} %get-tuple-element.50), channel_id=1, source_target_pairs={{0,8},{4,12},{8,0},{12,4},{16,24},{20,28},{24,16},{28,20},{32,40},... | collective-permute-start | bytes 56 | tf_op jit(solution)/shard_map/ppermute | solution.py:30
  19.2 3.9 %collective-permute-start.5 = (f32[4]{0:T(128)S(1)}, f32[4]{0:T(128)S(1)}, u32[]{:S(2)}, u32[]{:S(2)}) collective-permute-start(f32[4]{0:T(128)S(1)} %get-tuple-element.55), channel_id=1, source_target_pairs={{0,16},{4,20},{8,24},{12,28},{16,0},{20,4},{24,8},{28,12},{32,48},... | collective-permute-start | bytes 56 | tf_op jit(solution)/shard_map/ppermute | solution.py:30
  23.6 2.4 %collective-permute-start.7 = (f32[4]{0:T(128)S(1)}, f32[4]{0:T(128)S(1)}, u32[]{:S(2)}, u32[]{:S(2)}) collective-permute-start(f32[4]{0:T(128)S(1)} %get-tuple-element.45), channel_id=1, source_target_pairs={{0,32},{4,36},{8,40},{12,44},{16,48},{20,52},{24,56},{28,60},{32,0... | collective-permute-start | bytes 56 | tf_op jit(solution)/shard_map/ppermute | solution.py:30
  26.6 3.3 %collective-permute-start.9 = (f32[4]{0:T(128)S(1)}, f32[4]{0:T(128)S(1)}, u32[]{:S(2)}, u32[]{:S(2)}) collective-permute-start(f32[4]{0:T(128)S(1)} %get-tuple-element.43), channel_id=1, source_target_pairs={{0,64},{4,68},{8,72},{12,76},{16,80},{20,84},{24,88},{28,92},{32,9... | collective-permute-start | bytes 56 | tf_op jit(solution)/shard_map/ppermute | solution.py:30
  79.8 6.0 %copy-start.10 = (f32[4]{0:T(128)S(1)}, f32[4]{0:T(128)}, u32[]{:S(2)}) copy-start(f32[4]{0:T(128)} %copy-done.9) | copy-start | bytes 52
  79.8 6.0 %copy-start.14 = (f32[4]{0:T(128)S(1)}, f32[4]{0:T(128)}, u32[]{:S(2)}) copy-start(f32[4]{0:T(128)} %get-tuple-element.54) | copy-start | bytes 52
  79.8 6.0 %copy-start.15 = (f32[4]{0:T(128)S(1)}, f32[4]{0:T(128)}, u32[]{:S(2)}) copy-start(f32[4]{0:T(128)} %get-tuple-element.5) | copy-start | bytes 52
  79.8 6.0 %copy-start.16 = (f32[4]{0:T(128)S(1)}, f32[4]{0:T(128)}, u32[]{:S(2)}) copy-start(f32[4]{0:T(128)} %get-tuple-element.51) | copy-start | bytes 52
  79.8 6.0 %copy-start.17 = (f32[4]{0:T(128)S(1)}, f32[4]{0:T(128)}, u32[]{:S(2)}) copy-start(f32[4]{0:T(128)} %get-tuple-element.41) | copy-start | bytes 52
  79.8 6.0 %copy-start.18 = (f32[4]{0:T(128)S(1)}, f32[4]{0:T(128)}, u32[]{:S(2)}) copy-start(f32[4]{0:T(128)} %get-tuple-element.42) | copy-start | bytes 52
  79.8 8.4 %slice-start = ((f32[4,2]{0,1:T(2,128)}), f32[4,1]{0,1:T(1,128)S(1)}, s32[]{:S(2)}) async-start(f32[4,2]{0,1:T(2,128)} %copy-done.19), calls=%async_computation.3 | async-start | bytes 1024 | tf_op jit(solution)/shard_map/slice | solution.py:83
  83.6 3.9 %copy-start.1 = (bf16[512,128]{1,0:T(8,128)(2,1)}, bf16[512,128]{1,0:T(8,128)(2,1)S(1)}, u32[]{:S(2)}) copy-start(bf16[512,128]{1,0:T(8,128)(2,1)S(1)} %convolution_convert_fusion.3) | copy-start | bytes 393220
  87.5 18.1 %copy-start.5 = (f32[4,512]{1,0:T(4,128)S(1)}, f32[4,512]{1,0:T(4,128)}, u32[]{:S(2)}) copy-start(f32[4,512]{1,0:T(4,128)} %get-tuple-element.33) | copy-start | bytes 24580
  87.5 8.5 %collective-permute-start = (bf16[4,128,128]{2,1,0:T(8,128)(2,1)}, bf16[4,128,128]{2,1,0:T(8,128)(2,1)S(1)}, u32[]{:S(2)}, u32[]{:S(2)}) collective-permute-start(bf16[4,128,128]{2,1,0:T(8,128)(2,1)} %get-tuple-element.57), channel_id=1, source_target_pairs={{0,4},{4,0},{8,12},{12,8},{16,20},{20,16},{24,28},{28,24},{32,36},... | collective-permute-start | bytes 393224 | tf_op jit(solution)/shard_map/ppermute | solution.py:30
  88.3 20.3 %copy-start.7 = (f32[4]{0:T(128)S(1)}, f32[4]{0:T(128)}, u32[]{:S(2)}) copy-start(f32[4]{0:T(128)} %get-tuple-element.49) | copy-start | bytes 52
  88.4 20.3 %copy-start.8 = (f32[4]{0:T(128)S(1)}, f32[4]{0:T(128)}, u32[]{:S(2)}) copy-start(f32[4]{0:T(128)} %get-tuple-element.56) | copy-start | bytes 52
  88.4 20.3 %copy-start.12 = (f32[4]{0:T(128)S(1)}, f32[4]{0:T(128)}, u32[]{:S(2)}) copy-start(f32[4]{0:T(128)} %get-tuple-element.46) | copy-start | bytes 52
  91.2 19.1 %copy-start.4 = (f32[4,512]{1,0:T(4,128)S(1)}, f32[4,512]{1,0:T(4,128)}, u32[]{:S(2)}) copy-start(f32[4,512]{1,0:T(4,128)} %get-tuple-element.32) | copy-start | bytes 24580
  93.2 19.6 %copy-start.11 = (f32[4]{0:T(128)S(1)}, f32[4]{0:T(128)}, u32[]{:S(2)}) copy-start(f32[4]{0:T(128)} %get-tuple-element.44) | copy-start | bytes 52
  93.4 21.8 %copy-start.3 = (f32[4,512]{1,0:T(4,128)S(1)}, f32[4,512]{1,0:T(4,128)}, u32[]{:S(2)}) copy-start(f32[4,512]{1,0:T(4,128)} %get-tuple-element.31) | copy-start | bytes 24580
  96.0 23.1 %copy-start.13 = (f32[4]{0:T(128)S(1)}, f32[4]{0:T(128)}, u32[]{:S(2)}) copy-start(f32[4]{0:T(128)} %get-tuple-element.53) | copy-start | bytes 52
  96.8 28.0 %copy-start.2 = (f32[4,512]{1,0:T(4,128)S(1)}, f32[4,512]{1,0:T(4,128)}, u32[]{:S(2)}) copy-start(f32[4,512]{1,0:T(4,128)} %get-tuple-element.30) | copy-start | bytes 24580
  96.8 5.2 %collective-permute-start.2 = (bf16[4,128,128]{2,1,0:T(8,128)(2,1)S(1)}, bf16[4,128,128]{2,1,0:T(8,128)(2,1)S(1)}, u32[]{:S(2)}, u32[]{:S(2)}) collective-permute-start(bf16[4,128,128]{2,1,0:T(8,128)(2,1)S(1)} %fusion.74), channel_id=1, source_target_pairs={{0,8},{4,12},{8,0},{12,4},{16,24},{20,28},{24,16},{28,20},{32,40},... | collective-permute-start | bytes 393224 | tf_op jit(solution)/shard_map/ppermute | solution.py:30
  102.8 5.8 %collective-permute-start.4 = (bf16[4,128,128]{2,1,0:T(8,128)(2,1)S(1)}, bf16[4,128,128]{2,1,0:T(8,128)(2,1)S(1)}, u32[]{:S(2)}, u32[]{:S(2)}) collective-permute-start(bf16[4,128,128]{2,1,0:T(8,128)(2,1)S(1)} %fusion.43), channel_id=1, source_target_pairs={{0,16},{4,20},{8,24},{12,28},{16,0},{20,4},{24,8},{28,12},{32,48},... | collective-permute-start | bytes 393224 | tf_op jit(solution)/shard_map/ppermute | solution.py:30
  108.9 18.9 %copy-start.6 = (f32[4,512]{1,0:T(4,128)S(1)}, f32[4,512]{1,0:T(4,128)}, u32[]{:S(2)}) copy-start(f32[4,512]{1,0:T(4,128)} %get-tuple-element.28) | copy-start | bytes 24580
  108.9 3.9 %collective-permute-start.6 = (bf16[4,128,128]{2,1,0:T(8,128)(2,1)S(1)}, bf16[4,128,128]{2,1,0:T(8,128)(2,1)S(1)}, u32[]{:S(2)}, u32[]{:S(2)}) collective-permute-start(bf16[4,128,128]{2,1,0:T(8,128)(2,1)S(1)} %get-tuple-element.9), channel_id=1, source_target_pairs={{0,32},{4,36},{8,40},{12,44},{16,48},{20,52},{24,56},{28,60},{32,0... | collective-permute-start | bytes 393224 | tf_op jit(solution)/shard_map/ppermute | solution.py:30
  112.9 6.2 %collective-permute-start.8 = (bf16[4,128,128]{2,1,0:T(8,128)(2,1)S(1)}, bf16[4,128,128]{2,1,0:T(8,128)(2,1)S(1)}, u32[]{:S(2)}, u32[]{:S(2)}) collective-permute-start(bf16[4,128,128]{2,1,0:T(8,128)(2,1)S(1)} %fusion.42), channel_id=1, source_target_pairs={{0,64},{4,68},{8,72},{12,76},{16,80},{20,84},{24,88},{28,92},{32,9... | collective-permute-start | bytes 393224 | tf_op jit(solution)/shard_map/ppermute | solution.py:30
  119.3 8.0 %collective-permute-start.10 = (bf16[4,128,128]{2,1,0:T(8,128)(2,1)S(1)}, bf16[4,128,128]{2,1,0:T(8,128)(2,1)S(1)}, u32[]{:S(2)}, u32[]{:S(2)}) collective-permute-start(bf16[4,128,128]{2,1,0:T(8,128)(2,1)S(1)} %fusion.39), channel_id=1, source_target_pairs={{0,128},{4,132},{8,136},{12,140},{16,144},{20,148},{24,152},{28,15... | collective-permute-start | bytes 393224 | tf_op jit(solution)/shard_map/ppermute | solution.py:30
Sparse Core Ops, SparseCore 0:
  9.2 54.6 all-gather.1
  136.1 54.3 reduce-scatter.1

commit v2 on v1

v2 whole, which is shorter than its diff:
```python
import jax
import jax.numpy as jnp
from jax import lax
from jax.experimental import pallas as pl
from jax.experimental.pallas import tpu as pltpu
from jax.sharding import PartitionSpec as P

BLOCK = 128
F32 = jnp.float32
BF16 = jnp.bfloat16
MESH = pl.DeviceIdType.MESH
NEVER = -1e30
HEADS = 4
SIZE = 128
LEVELS = 9
ROWS = 512
BLOCKS = ROWS // BLOCK
PART = 1024
BITS = 6


def dot(a, b):
    return jnp.dot(a, b, preferred_element_type=F32)


def dot_t(a, b):
    return lax.dot_general(a, b, (((1,), (1,)), ((), ())), preferred_element_type=F32)


def split3(wide):
    high = wide.astype(BF16)
    rest = wide - high.astype(F32)
    middle = rest.astype(BF16)
    low = (rest - middle.astype(F32)).astype(BF16)
    return high, middle, low


def softplus(x):
    return jnp.maximum(x, 0.0) + jnp.log1p(jnp.exp(-jnp.abs(x)))


def kernel(
    x_ref, ld_ref, wq_ref, wk_ref, wv_ref, wl_ref, wo_ref, out_ref,
    xg, wq, wkv, wo, ng,
    ldp, d36, dect, ends, offs, gsend, grecv, coef,
    qb, kb, vb, fac, acc, qs, sb, sb16, run, ssend, bkt,
    tok_s, tok_r, dec_s, dec_r, st_s, st_r, fw_s, fw_r, wo_s, wo_r, nm_s, nm_r, loc,
):
    y = lax.axis_index("tp")
    s = lax.axis_index("seq")
    core = lax.rem(s, 2)
    cx = lax.rem(lax.div(s, 2), 4)
    cz = lax.div(s, 8)
    right, left, across = lax.rem(y + 1, 4), lax.rem(y + 3, 4), lax.rem(y + 2, 4)
    to_right, to_left, to_across = {"tp": right}, {"tp": left}, {"tp": across}
    uppers = [core, lax.rem(cx, 2), lax.div(cx, 2), lax.rem(cz, 2), lax.rem(lax.div(cz, 2), 2), lax.div(cz, 4)]
    mates = [
        s + 1 - 2 * core,
        s + (1 - 2 * uppers[1]) * 2,
        s + (3 - 2 * cx) * 2,
        s + (1 - 2 * uppers[3]) * 8,
        s + (1 - 2 * uppers[4]) * 16,
    ]
    mates = [{"seq": m} for m in mates]
    is_top = cz >= 4
    is_source = jnp.logical_or(cz == 0, cz == 3)
    plane = lax.rem(s, 8)
    near = {"seq": jnp.where(cz == 0, 56, 32) + plane}
    far = {"seq": jnp.where(cz == 0, 48, 40) + plane}
    source = {"seq": jnp.where(cz < 6, 24, 0) + plane}

    def remote(src, dst, send, recv, device):
        return pltpu.make_async_remote_copy(
            src_ref=src, dst_ref=dst, send_sem=send, recv_sem=recv, device_id=device, device_id_type=MESH
        )

    locals_ = [
        pltpu.make_async_copy(x_ref, xg.at[y], loc.at[0]),
        pltpu.make_async_copy(wk_ref, wkv.at[:, pl.ds(0, SIZE)], loc.at[1]),
        pltpu.make_async_copy(wv_ref, wkv.at[:, pl.ds(SIZE, SIZE)], loc.at[2]),
        pltpu.make_async_copy(wq_ref, wq, loc.at[3]),
    ]
    own_out = pltpu.make_async_copy(wo_ref.at[:, pl.ds(pl.multiple_of(y * PART, PART), PART)], wo.at[y], loc.at[5])
    for c in locals_:
        c.start()

    @pl.when(jnp.logical_not(is_top))
    def _():
        bkt[BITS - 1] = jnp.zeros((HEADS * SIZE, SIZE), BF16)

    barrier = pltpu.get_barrier_semaphore()
    for peer in [to_right, to_left, to_across] + mates:
        pl.semaphore_signal(barrier, inc=1, device_id=peer, device_id_type=MESH)

    @pl.when(is_top)
    def _():
        pl.semaphore_signal(barrier, inc=1, device_id=source, device_id_type=MESH)

    pl.semaphore_wait(barrier, 3 + len(mates) + jnp.where(is_source, 2, 0))

    half = BLOCK // 2

    def own_rows(r, side):
        rows = pl.ds(pl.multiple_of(r * BLOCK, BLOCK), BLOCK)
        i = 2 * r + side
        return remote(x_ref.at[rows], xg.at[y, rows], tok_s.at[i], tok_r.at[i], to_left if side else to_right)

    def onward(r, side):
        rows = pl.ds(pl.multiple_of(r * BLOCK + side * half, half), half)
        i = 2 * BLOCKS + 2 * r + side
        owner = right if side else left
        return remote(xg.at[owner, rows], xg.at[owner, rows], tok_s.at[i], tok_r.at[i], to_left if side else to_right)

    for r in range(BLOCKS):
        own_rows(r, 0).start()
        own_rows(r, 1).start()

    def pass_on(r):
        for side in range(2):
            own_rows(r, side).wait_recv()
            onward(r, side).start()

    ldp[...] = jnp.zeros_like(ldp)
    ldp[0:HEADS, :] = ld_ref[...]
    row = lax.broadcasted_iota(jnp.int32, (ROWS, ROWS), 0)
    col = lax.broadcasted_iota(jnp.int32, (ROWS, ROWS), 1)
    lower = (row >= col).astype(F32).astype(BF16)
    upper_tri = (row <= col).astype(F32).astype(BF16)
    wide_row = lax.broadcasted_iota(jnp.int32, (BLOCK, HEADS * LEVELS), 0)
    wide_col = lax.broadcasted_iota(jnp.int32, (BLOCK, HEADS * LEVELS), 1)
    spread = (lax.div(wide_col, LEVELS) == wide_row).astype(F32).astype(BF16)
    level_of = lax.rem(lax.broadcasted_iota(jnp.int32, (8, HEADS * LEVELS), 1), LEVELS)
    spread_decay = sum(dot(lower, dot(p, spread).astype(BF16)) for p in split3(jnp.transpose(ldp[...])))
    d36[...] = spread_decay
    along = sum(dot(p, upper_tri) for p in split3(ldp[0:16, :]))
    dect[...] = along[0:8]
    for c in range(BLOCKS):
        last = (c + 1) * BLOCK - 1
        ends[c] = jnp.broadcast_to(dect[:, last : last + 1], (8, SIZE))
    gsend[0] = jnp.zeros((16, SIZE), F32)
    gsend[0, 0:8] = ends[BLOCKS - 1]
    gsend[0, 8:16, 0 : HEADS * LEVELS] = jnp.broadcast_to(d36[ROWS - 1 : ROWS, :], (8, HEADS * LEVELS))
    before = jnp.zeros((8, HEADS * LEVELS), F32)
    gap_off = jnp.zeros((8, HEADS * LEVELS), F32)
    decay_copies = []
    for bit in range(BITS - 1):
        if bit == 2:
            pass_on(0)
        up = uppers[bit].astype(F32)
        c = remote(gsend.at[bit], grecv.at[bit], dec_s.at[bit], dec_r.at[bit], mates[bit])
        c.start()
        c.wait_recv()
        decay_copies.append(c)
        mine = gsend[bit]
        other = grecv[bit]
        coef[bit, 0] = up + (1.0 - up) * jnp.exp(other[0:8])
        coef[bit, 1] = up * jnp.exp(mine[0:8]) + (1.0 - up)
        gap_off = gap_off + jnp.where(level_of == 3 + bit, up * before + (1.0 - up) * NEVER, 0.0)
        before = before + up * other[8:16, 0 : HEADS * LEVELS]
        if bit < BITS - 2:
            gsend[bit + 1] = mine + other
    up = uppers[BITS - 1].astype(F32)
    gap_off = gap_off + jnp.where(level_of == 3 + BITS - 1, up * before + (1.0 - up) * NEVER, 0.0)
    offs[...] = gap_off
    for c in locals_:
        c.wait()

    def project(r, weights):
        rows = pl.ds(pl.multiple_of(r * BLOCK, BLOCK), BLOCK)
        return sum(dot(xg[i, rows, :], weights[i * PART : (i + 1) * PART, :]) for i in range(4))

    def keys_part(r):
        rows = pl.ds(pl.multiple_of(r * BLOCK, BLOCK), BLOCK)
        both = project(r, wkv)
        values = both[:, SIZE:].astype(BF16)
        kb[rows, :] = both[:, :SIZE].astype(BF16)
        vb[rows, :] = values
        k_t = jnp.transpose(both[:, :SIZE].astype(BF16).astype(F32))
        weight = jnp.exp(ends[r] - dect[:, rows])
        for h in range(HEADS):
            scaled = (k_t * weight[h : h + 1, :]).astype(BF16)
            sb[r, h * SIZE : (h + 1) * SIZE, :] = dot(scaled, values)

    def fade_of(c, before_c, h):
        return jnp.exp(ends[c] - ends[before_c])[h : h + 1, :]

    def query_part(r):
        rows = pl.ds(pl.multiple_of(r * BLOCK, BLOCK), BLOCK)
        qb[rows, :] = project(r, wq).astype(BF16)
        weight = softplus(
            sum(dot_t(xg[i, rows, :], wl_ref[:, i * PART : (i + 1) * PART]) for i in range(4))
        )
        previous = jnp.maximum(r - 1, 0)
        last = d36[pl.ds(previous * BLOCK + BLOCK - 1, 1), :]
        second = d36[2 * BLOCK - 1 : 2 * BLOCK, :]
        odd = lax.rem(r, 2).astype(F32)
        late = lax.div(r, 2).astype(F32)
        kind = level_of[0:1]
        off = jnp.where(kind == 1, odd * -last + (1.0 - odd) * NEVER, offs[0:1, :])
        off = jnp.where(kind == 2, late * -second + (1.0 - late) * NEVER, off)
        here = d36[rows, :]
        power = jnp.where(kind == 0, 0.0, here + off)
        factor = weight * jnp.exp(power)
        fac[rows, :] = factor
        keys = kb[rows, :]
        values = vb[rows, :]
        inside_row = lax.broadcasted_iota(jnp.int32, (BLOCK, BLOCK), 0)
        inside_col = lax.broadcasted_iota(jnp.int32, (BLOCK, BLOCK), 1)
        causal = inside_row >= inside_col
        along_here = dect[:, rows]
        for h in range(HEADS):
            cols = slice(h * SIZE, (h + 1) * SIZE)
            query = qb[rows, cols]
            wide = query.astype(F32)
            scores = dot_t(query, keys)
            gap = here[:, h * LEVELS : h * LEVELS + 1] - along_here[h : h + 1, :]
            mixing = jnp.exp(jnp.where(causal, gap, NEVER)) * scores * factor[:, h * LEVELS : h * LEVELS + 1]
            total = dot(mixing.astype(BF16), values)
            near_query = (wide * factor[:, h * LEVELS + 1 : h * LEVELS + 2]).astype(BF16)
            total = total + dot(near_query, sb[previous, cols, :].astype(BF16))
            late_query = (wide * factor[:, h * LEVELS + 2 : h * LEVELS + 3]).astype(BF16)
            total = total + dot(late_query, sb16[cols, :])
            acc[rows, cols] = total
            for bit in range(BITS):
                at = h * LEVELS + 3 + bit
                qs[bit, rows, cols] = (wide * factor[:, at : at + 1]).astype(BF16)

    def pair_sum():
        for h in range(HEADS):
            cols = slice(h * SIZE, (h + 1) * SIZE)
            sb16[cols, :] = (sb[1, cols, :] + fade_of(1, 0, h) * sb[0, cols, :]).astype(BF16)

    sb16[...] = jnp.zeros_like(sb16)

    for r in range(BLOCKS - 1):
        pass_on(r + 1)
        onward(r, 0).wait_recv()
        onward(r, 1).wait_recv()
        keys_part(r)
        if r == 1:
            pair_sum()
        query_part(jnp.int32(r))
    tail = BLOCKS - 1
    onward(tail, 0).wait_recv()
    onward(tail, 1).wait_recv()
    keys_part(tail)
    for h in range(HEADS):
        cols = slice(h * SIZE, (h + 1) * SIZE)
        first = sb[1, cols, :] + fade_of(1, 0, h) * sb[0, cols, :]
        second = sb[3, cols, :] + fade_of(3, 2, h) * sb[2, cols, :]
        whole = second + fade_of(3, 1, h) * first
        run[cols, :] = whole
        ssend[0, cols, :] = whole.astype(BF16)

    mine = pl.ds(pl.multiple_of(core * 2 * SIZE, 2 * SIZE), 2 * SIZE)
    state_copies = []
    hand_overs = []
    c = remote(ssend.at[0], bkt.at[0], st_s.at[0], st_r.at[0], mates[0])
    c.start()
    state_copies.append(c)

    wide_half = pl.ds(pl.multiple_of(core * 256, 256), 256)
    own_out.start()
    weight_copies = []
    for i, (peer, device) in enumerate(((right, to_right), (left, to_left), (across, to_across))):
        c = remote(
            wo_ref.at[wide_half, pl.ds(pl.multiple_of(peer * PART, PART), PART)],
            wo.at[y, wide_half], wo_s.at[i], wo_r.at[i], device,
        )
        c.start()
        weight_copies.append(c)

    query_part(jnp.int32(tail))

    def take(bit):
        for h in range(HEADS):
            cols = slice(h * SIZE, (h + 1) * SIZE)
            acc[:, cols] += dot(qs[bit, :, cols], bkt[bit, cols, :])

    state_copies[0].wait_recv()
    for bit in range(BITS):
        for i in range(2):
            one = pl.ds(pl.multiple_of((core * 2 + i) * SIZE, SIZE), SIZE)
            if bit < BITS - 1:
                head = pl.ds(core * 2 + i, 1)
                merged = coef[bit, 0, head, :] * run[one, :] + coef[bit, 1, head, :] * bkt[bit, one, :].astype(F32)
                run[one, :] = merged
                ssend[bit + 1, one, :] = merged.astype(BF16)
        nxt = bit + 1
        if nxt < BITS - 1:
            c = remote(ssend.at[nxt, mine], bkt.at[nxt, mine], st_s.at[nxt], st_r.at[nxt], mates[nxt])
            c.start()
            state_copies.append(c)
        elif nxt == BITS - 1:

            @pl.when(is_source)
            def _():
                remote(ssend.at[nxt, mine], bkt.at[nxt, mine], st_s.at[nxt], st_r.at[nxt], near).start()
                remote(ssend.at[nxt, mine], bkt.at[nxt, mine], st_s.at[nxt + 1], st_r.at[nxt], far).start()

        if bit > 0 and bit < BITS - 1:
            hand = remote(bkt.at[bit, mine], bkt.at[bit, mine], fw_s.at[bit], fw_r.at[bit], mates[0])
            hand.start()
            hand_overs.append(hand)
        if bit == 0:
            take(0)
        elif bit > 1:
            hand_overs[bit - 2].wait_recv()
            take(bit - 1)
        if nxt < BITS - 1:
            state_copies[nxt].wait_recv()
        elif nxt == BITS - 1:
            final = remote(bkt.at[nxt, mine], bkt.at[nxt, mine], fw_s.at[nxt], fw_r.at[nxt], mates[0])

            @pl.when(is_top)
            def _():
                remote(ssend.at[nxt, mine], bkt.at[nxt, mine], st_s.at[nxt], st_r.at[nxt], source).wait_recv()
                final.start()

            @pl.when(is_top)
            def _():
                final.wait_recv()

    def own_normed(r, side):
        rows = pl.ds(r * BLOCK, BLOCK)
        i = 2 * r + side
        return remote(ng.at[y, rows], ng.at[y, rows], nm_s.at[i], nm_r.at[i], to_left if side else to_right)

    def onward_normed(r, side):
        rows = pl.ds(r * BLOCK + side * half, half)
        i = 2 * BLOCKS + 2 * r + side
        owner = right if side else left
        return remote(ng.at[owner, rows], ng.at[owner, rows], nm_s.at[i], nm_r.at[i], to_left if side else to_right)

    for r in range(BLOCKS):
        rows = slice(r * BLOCK, (r + 1) * BLOCK)
        for h in range(HEADS):
            cols = slice(h * SIZE, (h + 1) * SIZE)
            value = acc[rows, cols] + dot(qs[BITS - 1, rows, cols], bkt[BITS - 1, cols, :])
            mean = jnp.mean(value * value, axis=-1, keepdims=True)
            ng[y, rows, cols] = (value * lax.rsqrt(mean + 1e-05)).astype(BF16)
        own_normed(r, 0).start()
        own_normed(r, 1).start()

    share = []
    for i, owner in enumerate((left, right, across)):
        weight_copies[i].wait_recv()
        c = remote(wo.at[owner, wide_half], wo.at[owner, wide_half], wo_s.at[3 + i], wo_r.at[3 + i], mates[0])
        c.start()
        share.append(c)
    own_out.wait()

    def pass_normed(r):
        for side in range(2):
            own_normed(r, side).wait_recv()
            onward_normed(r, side).start()

    pass_normed(0)
    for c in share:
        c.wait_recv()
    for r in range(BLOCKS):
        if r + 1 < BLOCKS:
            pass_normed(r + 1)
        onward_normed(r, 0).wait_recv()
        onward_normed(r, 1).wait_recv()
        rows = slice(r * BLOCK, (r + 1) * BLOCK)
        out_ref[rows, :] = sum(dot(ng[i, rows, :], wo[i]) for i in range(4)).astype(BF16)

    for r in range(BLOCKS):
        for side in range(2):
            own_rows(r, side).wait_send()
            onward(r, side).wait_send()
            own_normed(r, side).wait_send()
            onward_normed(r, side).wait_send()
    for c in decay_copies + state_copies + hand_overs + weight_copies + share:
        c.wait_send()

    @pl.when(is_source)
    def _():
        last_bit = BITS - 1
        remote(ssend.at[last_bit, mine], bkt.at[last_bit, mine], st_s.at[last_bit], st_r.at[last_bit], near).wait_send()
        remote(ssend.at[last_bit, mine], bkt.at[last_bit, mine], st_s.at[last_bit + 1], st_r.at[last_bit], far).wait_send()

    @pl.when(is_top)
    def _():
        final.wait_send()


def body(tokens, log_decay, w_query, w_key, w_value, w_level, w_out):
    hbm = pl.BlockSpec(memory_space=pl.ANY)
    vmem = pl.BlockSpec(memory_space=pltpu.VMEM)
    dma = pltpu.SemaphoreType.DMA
    wide = HEADS * LEVELS
    return pl.pallas_call(
        kernel,
        name="layer",
        out_shape=pltpu.VMEM((ROWS, PART), BF16),
        in_specs=[hbm, vmem, hbm, hbm, hbm, vmem, hbm],
        out_specs=vmem,
        scratch_shapes=[
            pltpu.VMEM((4, ROWS, PART), BF16),
            pltpu.VMEM((4 * PART, HEADS * SIZE), BF16),
            pltpu.VMEM((4 * PART, 2 * SIZE), BF16),
            pltpu.VMEM((4, HEADS * SIZE, PART), BF16),
            pltpu.VMEM((4, ROWS, HEADS * SIZE), BF16),
            pltpu.VMEM((SIZE, ROWS), F32),
            pltpu.VMEM((ROWS, wide), F32),
            pltpu.VMEM((8, ROWS), F32),
            pltpu.VMEM((BLOCKS, 8, SIZE), F32),
            pltpu.VMEM((8, wide), F32),
            pltpu.VMEM((BITS - 1, 16, SIZE), F32),
            pltpu.VMEM((BITS - 1, 16, SIZE), F32),
            pltpu.VMEM((BITS - 1, 2, 8, SIZE), F32),
            pltpu.VMEM((ROWS, HEADS * SIZE), BF16),
            pltpu.VMEM((ROWS, SIZE), BF16),
            pltpu.VMEM((ROWS, SIZE), BF16),
            pltpu.VMEM((ROWS, wide), F32),
            pltpu.VMEM((ROWS, HEADS * SIZE), F32),
            pltpu.VMEM((BITS, ROWS, HEADS * SIZE), BF16),
            pltpu.VMEM((BLOCKS, HEADS * SIZE, SIZE), F32),
            pltpu.VMEM((HEADS * SIZE, SIZE), BF16),
            pltpu.VMEM((HEADS * SIZE, SIZE), F32),
            pltpu.VMEM((BITS, HEADS * SIZE, SIZE), BF16),
            pltpu.VMEM((BITS, HEADS * SIZE, SIZE), BF16),
            dma((4 * BLOCKS,)), dma((4 * BLOCKS,)),
            dma((BITS - 1,)), dma((BITS - 1,)),
            dma((BITS + 1,)), dma((BITS + 1,)),
            dma((BITS,)), dma((BITS,)),
            dma((6,)), dma((6,)),
            dma((4 * BLOCKS,)), dma((4 * BLOCKS,)),
            dma((6,)),
        ],
        compiler_params=pltpu.CompilerParams(
            collective_id=0, has_side_effects=True, vmem_limit_bytes=56 << 20
        ),
        cost_estimate=pl.CostEstimate(flops=7_000_000_000, bytes_accessed=14_000_000, transcendentals=400_000),
    )(tokens, log_decay.T, w_query, w_key, w_value, w_level.T, w_out)


def solution(mesh):
    in_specs = (
        P("seq", "tp"),
        P("seq", "tp"),
        P(None, "tp"),
        P(None, "tp"),
        P(None, "tp"),
        P(None, "tp"),
        P("tp", None),
    )
    return jax.shard_map(
        body, mesh=mesh, in_specs=in_specs, out_specs=P("seq", "tp"), check_vma=False
    )
```

time: 198 us -> 94.2 us (0.48)
  waiting for transfers between devices: 111 us -> 0 us
  Pallas kernels: 0 us -> 93.1 us
  matrix products: 36.4 us -> 0 us
  starting transfers between devices: 19.8 us -> 0 us
  between operations: 13.9 us -> 0.01 us
  local copies, waits for them, and re-layouts: 8.63 us -> 0.97 us
  other arithmetic: 7.64 us -> 0 us
    pallas_call x0 -> x1, Pallas kernels: none -> 93.1 us  [body(): pl.pallas_call(kernel, name='layer', out_shape=pltpu.VMEM((ROWS, PART), B...]
    reduce_scatter x1 -> x0, waiting for transfers between devices: 54.5 us -> none  [body(): lax.psum_scatter(partial.astype(BF16), 'tp', scatter_dimension=1, tiled=T...]
    dot_general x19 -> x0, matrix products: 36.4 us -> none  [the longest x5 23.2 us: body(): dot = lambda a, b: jnp.dot(a, b, preferred_element_type=F32)]
    all_gather x1 -> x0, waiting for transfers between devices: 33.4 us -> none  [body(): piece = lax.all_gather(tokens, 'tp', axis=1, tiled=True)]
    ppermute x11 -> x0, waiting for transfers between devices: 22.4 us -> none  [swap(): return lax.ppermute(x, 'seq', pairs)]
    ppermute x11 -> x0, starting transfers between devices: 19.8 us -> none  [swap(): return lax.ppermute(x, 'seq', pairs)]
    slice x11 -> x0, local copies, waits for them, and re-layouts: 3.18 us -> none  [the longest x1 1.23 us: body(): level[:, :, 1 + local_bits + bit] * jnp.exp(decay + befores[bit][None, :])]
    convert_element_type x7 -> x0, other arithmetic: 2.2 us -> none  [the longest x5 2.08 us: body(): other = swap(state.astype(BF16), bit)]
  transfers between devices with their start and end apart: 13 -> 0, of which waited for: 11 -> 0; matrix products, arithmetic and copies ran while one was open for 9% -> 0% of each run, Pallas kernels for 0% -> 0%
where the time goes in v2:
time: 94.2 us; the launch traced here: 94.1 us
  Pallas kernels  93.1 us (99%)
  local copies, waits for them, and re-layouts  0.97 us (1%)
    pallas_call x1, Pallas kernels, body(): pl.pallas_call(kernel, name='layer', out_shape=pltpu.VMEM((ROWS, PART), B...  93.1 us

profile of v2, /device:TPU:1, one launch (start us, length us, event | category | flops | bytes accessed | tf_op | source)
XLA Modules:
  0.0 94.1 jit_solution(11164197955173384477)
XLA Ops:
  0.0 93.1 %layer.1 = bf16[512,1024]{1,0:T(8,128)(2,1)S(1)} custom-call(bf16[512,1024]{1,0:T(8,128)(2,1)} %x_ref.1, f32[4,512]{1,0:T(4,128)} %bitcast.3, bf16[4096,512]{1,0:T(8,128)(2,1)} %wq_ref.1, bf16[4096,128]{1,0:T(8,128)(2,1)} %wk_ref.1, bf16[4096,128]{1,0:T(8,128)(2,1)} %wv_ref.1, bf16[36,4096]{1,0:T(8,128)(2,1)} %bitcast.2, bf16[512,4096]{1,0:T(8,128)(2,1)} %wo_ref.1), custom_call_target="tpu_custom_call" | custom-call | flops 7000000000 | bytes 14000000 | tf_op jit(solution)/shard_map/layer/pallas_call | solution.py:394
  93.1 1.0 %copy.9 = bf16[512,1024]{1,0:T(8,128)(2,1)} copy(bf16[512,1024]{1,0:T(8,128)(2,1)S(1)} %layer.1) | data formatting | bytes 2097152

commit v3 on v2

v3 whole, which is shorter than its diff:
```python
import jax
import jax.numpy as jnp
from jax import lax
from jax.experimental import pallas as pl
from jax.experimental.pallas import tpu as pltpu
from jax.sharding import PartitionSpec as P

BLOCK = 128
F32 = jnp.float32
BF16 = jnp.bfloat16
MESH = pl.DeviceIdType.MESH
NEVER = -1e30
HEADS = 4
SIZE = 128
LEVELS = 9
ROWS = 512
BLOCKS = ROWS // BLOCK
PART = 1024
BITS = 6


def dot(a, b):
    return jnp.dot(a, b, preferred_element_type=F32)


def dot_t(a, b):
    return lax.dot_general(a, b, (((1,), (1,)), ((), ())), preferred_element_type=F32)


def split3(wide):
    high = wide.astype(BF16)
    rest = wide - high.astype(F32)
    middle = rest.astype(BF16)
    low = (rest - middle.astype(F32)).astype(BF16)
    return high, middle, low


def softplus(x):
    return jnp.maximum(x, 0.0) + jnp.log1p(jnp.exp(-jnp.abs(x)))


def kernel(
    x_ref, ld_ref, wq_ref, wk_ref, wv_ref, wl_ref, wo_ref, out_ref,
    xg, wq, wkv, wown, wop, ng, pacc,
    ldp, d36, dect, ends, offs, gsend, grecv, coef, pair, xin,
    qb, kb, vb, acc, qs, sb, sb16, run, ssend, bkt,
    tok_s, tok_r, dec_s, dec_r, st_s, st_r, xs, xr, fw_s, fw_r, wo_s, wo_r, nm_s, nm_r, loc,
):
    y = lax.axis_index("tp")
    s = lax.axis_index("seq")
    core = lax.rem(s, 2)
    cx = lax.rem(lax.div(s, 2), 4)
    cz = lax.div(s, 8)
    right, left, across = lax.rem(y + 1, 4), lax.rem(y + 3, 4), lax.rem(y + 2, 4)
    to_right, to_left, to_across = {"tp": right}, {"tp": left}, {"tp": across}
    uppers = [core, lax.rem(cx, 2), lax.div(cx, 2), lax.rem(cz, 2), lax.rem(lax.div(cz, 2), 2), lax.div(cz, 4)]
    mates = [
        s + 1 - 2 * core,
        s + (1 - 2 * uppers[1]) * 2,
        s + (3 - 2 * cx) * 2,
        s + (1 - 2 * uppers[3]) * 8,
        s + (1 - 2 * uppers[4]) * 16,
    ]
    opposite = {"seq": s + (1 - 2 * uppers[5]) * 32}
    x_across = {"seq": s + (1 - 2 * uppers[2]) * 4}
    mates = [{"seq": m} for m in mates]
    is_top = cz >= 4
    is_source = jnp.logical_or(cz == 0, cz == 3)
    plane = lax.rem(s, 8)
    near = {"seq": jnp.where(cz == 0, 56, 32) + plane}
    far = {"seq": jnp.where(cz == 0, 48, 40) + plane}
    source = {"seq": jnp.where(cz < 6, 24, 0) + plane}

    def remote(src, dst, send, recv, device):
        return pltpu.make_async_remote_copy(
            src_ref=src, dst_ref=dst, send_sem=send, recv_sem=recv, device_id=device, device_id_type=MESH
        )

    locals_ = [
        pltpu.make_async_copy(x_ref, xg.at[y], loc.at[0]),
        pltpu.make_async_copy(wk_ref, wkv.at[:, pl.ds(0, SIZE)], loc.at[1]),
        pltpu.make_async_copy(wv_ref, wkv.at[:, pl.ds(SIZE, SIZE)], loc.at[2]),
        pltpu.make_async_copy(wq_ref, wq, loc.at[3]),
    ]
    own_out = pltpu.make_async_copy(wo_ref.at[:, pl.ds(pl.multiple_of(y * PART, PART), PART)], wown, loc.at[4])
    for c in locals_:
        c.start()

    @pl.when(jnp.logical_not(is_top))
    def _():
        bkt[BITS - 1] = jnp.zeros((HEADS * SIZE, SIZE), BF16)

    barrier = pltpu.get_barrier_semaphore()
    for peer in [to_right, to_left, to_across, opposite, x_across] + mates:
        pl.semaphore_signal(barrier, inc=1, device_id=peer, device_id_type=MESH)

    @pl.when(is_top)
    def _():
        pl.semaphore_signal(barrier, inc=1, device_id=source, device_id_type=MESH)

    pl.semaphore_wait(barrier, 5 + len(mates) + jnp.where(is_source, 2, 0))

    half = BLOCK // 2

    def own_rows(r, side):
        rows = pl.ds(pl.multiple_of(r * BLOCK, BLOCK), BLOCK)
        i = 2 * r + side
        return remote(x_ref.at[rows], xg.at[y, rows], tok_s.at[i], tok_r.at[i], to_left if side else to_right)

    def onward(r, side):
        rows = pl.ds(pl.multiple_of(r * BLOCK + side * half, half), half)
        i = 2 * BLOCKS + 2 * r + side
        owner = right if side else left
        return remote(xg.at[owner, rows], xg.at[owner, rows], tok_s.at[i], tok_r.at[i], to_left if side else to_right)

    wide_cols = pl.ds(pl.multiple_of(core * 512, 512), 512)
    cols_a = pl.ds(pl.multiple_of(core * 512, 256), 256)
    cols_b = pl.ds(pl.multiple_of(core * 512 + 256, 256), 256)
    piece = cx * 8 + cz

    def some_rows(start, count):
        return pl.ds(pl.multiple_of(start * 16, 16), count * 16)

    def spread_copy(i, rows, cols, device):
        part = wop.at[:, rows, cols]
        return remote(part, part, wo_s.at[i], wo_r.at[i], device)

    fetch = []
    for i, (peer, device) in enumerate(((right, to_right), (left, to_left), (across, to_across))):
        there = pl.ds(pl.multiple_of(peer * PART + core * 512, 512), 512)
        rows = some_rows(piece, 1)
        fetch.append(remote(wo_ref.at[rows, there], wop.at[i, rows, wide_cols], wo_s.at[i], wo_r.at[i], device))
    over_z = [
        spread_copy(3, some_rows(piece, 1), wide_cols, mates[3]),
        spread_copy(4, some_rows(piece - lax.rem(cz, 2), 2), wide_cols, mates[4]),
        spread_copy(5, some_rows(piece - lax.rem(cz, 4), 4), wide_cols, opposite),
    ]
    over_x = [
        spread_copy(6, some_rows(cx * 8, 8), cols_a, mates[1]),
        spread_copy(7, some_rows(cx * 8, 8), cols_b, mates[2]),
    ]
    over_x2 = [
        spread_copy(8, some_rows(lax.div(cx, 2) * 16, 16), cols_a, mates[2]),
        spread_copy(9, some_rows(cx * 8, 8), cols_b, mates[1]),
        spread_copy(10, some_rows((3 - cx) * 8, 8), cols_b, mates[1]),
    ]
    share = spread_copy(11, pl.ds(0, ROWS), wide_cols, mates[0])
    for c in fetch:
        c.start()

    half = BLOCK // 2

    def own_rows(r, side):
        rows = pl.ds(r * BLOCK, BLOCK)
        i = 2 * r + side
        return remote(x_ref.at[rows], xg.at[y, rows], tok_s.at[i], tok_r.at[i], to_left if side else to_right)

    def onward(r, side):
        rows = pl.ds(r * BLOCK + side * half, half)
        i = 2 * BLOCKS + 2 * r + side
        owner = right if side else left
        return remote(xg.at[owner, rows], xg.at[owner, rows], tok_s.at[i], tok_r.at[i], to_left if side else to_right)

    for r in range(3):
        own_rows(r, 0).start()
        own_rows(r, 1).start()

    def pass_on(r):
        for side in range(2):
            own_rows(r, side).wait_recv()
            onward(r, side).start()
            if r + 3 < BLOCKS:
                own_rows(r + 3, side).start()

    ldp[...] = jnp.zeros_like(ldp)
    ldp[0:HEADS, :] = ld_ref[...]
    row = lax.broadcasted_iota(jnp.int32, (ROWS, ROWS), 0)
    col = lax.broadcasted_iota(jnp.int32, (ROWS, ROWS), 1)
    lower = (row >= col).astype(F32).astype(BF16)
    upper_tri = (row <= col).astype(F32).astype(BF16)
    wide_row = lax.broadcasted_iota(jnp.int32, (BLOCK, HEADS * LEVELS), 0)
    wide_col = lax.broadcasted_iota(jnp.int32, (BLOCK, HEADS * LEVELS), 1)
    spread = (lax.div(wide_col, LEVELS) == wide_row).astype(F32).astype(BF16)
    level_of = lax.rem(lax.broadcasted_iota(jnp.int32, (8, HEADS * LEVELS), 1), LEVELS)
    spread_decay = sum(dot(lower, dot(p, spread).astype(BF16)) for p in split3(jnp.transpose(ldp[...])))
    d36[...] = spread_decay
    along = sum(dot(p, upper_tri) for p in split3(ldp[0:16, :]))
    dect[...] = along[0:8]
    for c in range(BLOCKS):
        last = (c + 1) * BLOCK - 1
        ends[c] = jnp.broadcast_to(dect[:, last : last + 1], (8, SIZE))
    gsend[0] = jnp.zeros((24, SIZE), F32)
    gsend[0, 0:8] = ends[BLOCKS - 1]
    gsend[0, 8:16, 0 : HEADS * LEVELS] = jnp.broadcast_to(d36[ROWS - 1 : ROWS, :], (8, HEADS * LEVELS))
    before = jnp.zeros((8, HEADS * LEVELS), F32)
    gap_off = jnp.zeros((8, HEADS * LEVELS), F32)
    decay_copies = []
    for bit in range(BITS - 1):
        if bit == 2:
            for c in fetch:
                c.wait_recv()
            over_z[0].start()
        if bit == 3:
            over_z[0].wait_recv()
            over_z[1].start()
            pass_on(0)
        if bit == 4:
            over_z[1].wait_recv()
            over_z[2].start()
            pass_on(1)
        up = uppers[bit].astype(F32)
        c = remote(gsend.at[bit], grecv.at[bit], dec_s.at[bit], dec_r.at[bit], mates[bit])
        c.start()
        c.wait_recv()
        decay_copies.append(c)
        mine = gsend[bit]
        other = grecv[bit]
        coef[bit, 0] = up + (1.0 - up) * jnp.exp(other[0:8])
        coef[bit, 1] = up * jnp.exp(mine[0:8]) + (1.0 - up)
        gap_off = gap_off + jnp.where(level_of == 3 + bit, up * before + (1.0 - up) * NEVER, 0.0)
        before = before + up * other[8:16, 0 : HEADS * LEVELS]
        if bit < BITS - 2:
            gsend[bit + 1, 0:16] = mine[0:16] + other[0:16]
            gsend[bit + 1, 16:24] = mine[0:8]
        if bit == 2:
            third = other[16:24]
            fourth = other[0:8] - third
            side = uppers[1].astype(F32)
            pair[0] = side * jnp.exp(fourth) + (1.0 - side)
            pair[1] = side + (1.0 - side) * jnp.exp(third)
    up = uppers[BITS - 1].astype(F32)
    gap_off = gap_off + jnp.where(level_of == 3 + BITS - 1, up * before + (1.0 - up) * NEVER, 0.0)
    offs[...] = gap_off
    for c in locals_:
        c.wait()

    owners = (y, left, right, across)

    def project(r, weights, who=owners):
        rows = pl.ds(r * BLOCK, BLOCK)
        return sum(dot(xg[i, rows, :], weights[pl.ds(pl.multiple_of(i * PART, PART), PART), :]) for i in who)

    def keys_part(r):
        rows = pl.ds(r * BLOCK, BLOCK)
        part = project(r, wkv, owners[:3])
        onward(r, 0).wait_recv()
        onward(r, 1).wait_recv()
        both = part + project(r, wkv, owners[3:])
        values = both[:, SIZE:].astype(BF16)
        kb[rows, :] = both[:, :SIZE].astype(BF16)
        vb[rows, :] = values
        k_t = jnp.transpose(both[:, :SIZE].astype(BF16).astype(F32))
        weight = jnp.exp(ends[r] - dect[:, r * BLOCK : (r + 1) * BLOCK])
        for h in range(HEADS):
            scaled = (k_t * weight[h : h + 1, :]).astype(BF16)
            sb[r, h * SIZE : (h + 1) * SIZE, :] = dot(scaled, values)

    def fade_of(c, before_c, h):
        return jnp.exp(ends[c] - ends[before_c])[h : h + 1, :]

    def query_part(r):
        rows = slice(r * BLOCK, (r + 1) * BLOCK)
        qb[rows, :] = project(r, wq).astype(BF16)
        weight = softplus(sum(dot_t(xg[i, rows, :], wl_ref[:, i * PART : (i + 1) * PART]) for i in range(4)))
        kind = level_of[0:1]
        off = offs[0:1, :]
        off = jnp.where(kind == 1, -d36[r * BLOCK - 1 : r * BLOCK, :] if r % 2 else NEVER, off)
        off = jnp.where(kind == 2, -d36[2 * BLOCK - 1 : 2 * BLOCK, :] if r >= 2 else NEVER, off)
        here = d36[rows, :]
        power = jnp.where(kind == 0, 0.0, here + off)
        factor = weight * jnp.exp(power)
        keys = kb[rows, :]
        values = vb[rows, :]
        inside_row = lax.broadcasted_iota(jnp.int32, (BLOCK, BLOCK), 0)
        inside_col = lax.broadcasted_iota(jnp.int32, (BLOCK, BLOCK), 1)
        causal = inside_row >= inside_col
        along_here = dect[:, rows]
        for h in range(HEADS):
            cols = slice(h * SIZE, (h + 1) * SIZE)
            query = qb[rows, cols]
            wide = query.astype(F32)
            scores = dot_t(query, keys)
            gap = here[:, h * LEVELS : h * LEVELS + 1] - along_here[h : h + 1, :]
            mixing = jnp.exp(jnp.where(causal, gap, NEVER)) * scores * factor[:, h * LEVELS : h * LEVELS + 1]
            total = dot(mixing.astype(BF16), values)
            if r % 2:
                near_query = (wide * factor[:, h * LEVELS + 1 : h * LEVELS + 2]).astype(BF16)
                total = total + dot(near_query, sb[r - 1, cols, :].astype(BF16))
            if r >= 2:
                late_query = (wide * factor[:, h * LEVELS + 2 : h * LEVELS + 3]).astype(BF16)
                total = total + dot(late_query, sb16[cols, :])
            acc[rows, cols] = total
            for bit in range(BITS):
                at = h * LEVELS + 3 + bit
                qs[bit, rows, cols] = (wide * factor[:, at : at + 1]).astype(BF16)

    def pair_sum():
        for h in range(HEADS):
            cols = slice(h * SIZE, (h + 1) * SIZE)
            sb16[cols, :] = (sb[1, cols, :] + fade_of(1, 0, h) * sb[0, cols, :]).astype(BF16)

    pass_on(2)
    keys_part(0)
    over_z[2].wait_recv()
    for c in over_x:
        c.start()
    query_part(0)
    pass_on(3)
    keys_part(1)
    pair_sum()
    query_part(1)
    keys_part(2)
    keys_part(BLOCKS - 1)
    for h in range(HEADS):
        cols = slice(h * SIZE, (h + 1) * SIZE)
        first = sb[1, cols, :] + fade_of(1, 0, h) * sb[0, cols, :]
        second = sb[3, cols, :] + fade_of(3, 2, h) * sb[2, cols, :]
        whole = second + fade_of(3, 1, h) * first
        run[cols, :] = whole
        ssend[0, cols, :] = whole.astype(BF16)

    last_bit = BITS - 1

    def head_rows(wave):
        return pl.ds(pl.multiple_of((2 * wave + core) * SIZE, SIZE), SIZE)

    def state_copy(bit, wave):
        rows = pl.ds(2 * wave * SIZE, 2 * SIZE) if bit == 0 else head_rows(wave)
        i = 2 * bit + wave
        return remote(ssend.at[bit, rows], bkt.at[bit, rows], st_s.at[i], st_r.at[i], mates[bit])

    def top_copy(wave, device, place):
        rows = head_rows(wave)
        i = 2 * last_bit + wave
        return remote(ssend.at[last_bit, rows], bkt.at[last_bit, rows], st_s.at[i + 2 * place], st_r.at[i], device)

    def hand_over(bit, wave):
        rows = head_rows(wave)
        i = 2 * bit + wave
        return remote(bkt.at[bit, rows], bkt.at[bit, rows], fw_s.at[i], fw_r.at[i], mates[0])

    for wave in range(2):
        state_copy(0, wave).start()
    own_out.start()

    def take(bit):
        for h in range(HEADS):
            cols = slice(h * SIZE, (h + 1) * SIZE)
            acc[:, cols] += dot(qs[bit, :, cols], bkt[bit, cols, :])

    def corner(wave, third):
        rows = head_rows(wave)
        if third:
            return remote(ssend.at[1, rows], xin.at[0, rows], st_s.at[4 + wave], st_r.at[4 + wave], mates[2])
        return remote(ssend.at[1, rows], xin.at[1, rows], xs.at[wave], xr.at[wave], x_across)

    def scale(row, wave):
        return row[pl.ds(2 * wave + core, 1), :]

    def merge(bit, wave, other):
        one = head_rows(wave)
        return scale(coef.at[bit, 0], wave) * run[one, :] + scale(coef.at[bit, 1], wave) * other

    for wave in range(2):
        one = head_rows(wave)
        state_copy(0, wave).wait_recv()
        merged = merge(0, wave, bkt[0, one, :].astype(F32))
        run[one, :] = merged
        ssend[1, one, :] = merged.astype(BF16)
        corner(wave, False).start()
        state_copy(1, wave).start()
        corner(wave, True).start()
    query_part(2)
    for wave in range(2):
        one = head_rows(wave)
        state_copy(1, wave).wait_recv()
        corner(wave, True).wait_recv()
        corner(wave, False).wait_recv()
        run[one, :] = merge(1, wave, bkt[1, one, :].astype(F32))
        second = scale(pair.at[0], wave) * xin[0, one, :].astype(F32) + scale(pair.at[1], wave) * xin[1, one, :].astype(F32)
        merged = merge(2, wave, second)
        run[one, :] = merged
        ssend[3, one, :] = merged.astype(BF16)
        state_copy(3, wave).start()
        bkt[2, one, :] = second.astype(BF16)
        hand_over(1, wave).start()
        hand_over(2, wave).start()
    for c in over_x:
        c.wait_recv()
    for c in over_x2:
        c.start()
    query_part(BLOCKS - 1)
    for wave in range(2):
        one = head_rows(wave)
        state_copy(3, wave).wait_recv()
        merged = merge(3, wave, bkt[3, one, :].astype(F32))
        run[one, :] = merged
        ssend[4, one, :] = merged.astype(BF16)
        state_copy(4, wave).start()
        hand_over(3, wave).start()
    take(0)
    for wave in range(2):
        hand_over(1, wave).wait_recv()
    take(1)
    for wave in range(2):
        one = head_rows(wave)
        state_copy(4, wave).wait_recv()
        ssend[last_bit, one, :] = merge(4, wave, bkt[4, one, :].astype(F32)).astype(BF16)

        @pl.when(is_source)
        def _(wave=wave):
            top_copy(wave, near, 0).start()
            top_copy(wave, far, 1).start()

        hand_over(4, wave).start()
    for bit in (2, 3):
        for wave in range(2):
            hand_over(bit, wave).wait_recv()
        take(bit)

    many = ROWS // 2

    def own_normed(u, side):
        part = ng.at[y, u // 2, pl.ds(u % 2 * many, many)]
        i = 2 * u + side
        return remote(part, part, nm_s.at[i], nm_r.at[i], to_left if side else to_right)

    def onward_normed(u, side):
        part = ng.at[right if side else left, u // 2, pl.ds(u % 2 * many + side * BLOCK, BLOCK)]
        i = 8 + 2 * u + side
        return remote(part, part, nm_s.at[i], nm_r.at[i], to_left if side else to_right)

    for wave in range(2):

        @pl.when(is_top)
        def _(wave=wave):
            top_copy(wave, source, 0).wait_recv()
            hand_over(last_bit, wave).start()

    for wave in range(2):
        hand_over(last_bit - 1, wave).wait_recv()
    take(last_bit - 1)
    for wave in range(2):

        @pl.when(is_top)
        def _(wave=wave):
            hand_over(last_bit, wave).wait_recv()

        for part in range(2):
            rows = slice(part * many, (part + 1) * many)
            for i in range(2):
                h = 2 * wave + i
                cols = slice(h * SIZE, (h + 1) * SIZE)
                value = acc[rows, cols] + dot(qs[last_bit, rows, cols], bkt[last_bit, cols, :])
                mean = jnp.mean(value * value, axis=-1, keepdims=True)
                ng[y, wave, rows, i * SIZE : (i + 1) * SIZE] = (value * lax.rsqrt(mean + 1e-05)).astype(BF16)
            own_normed(2 * wave + part, 0).start()
            own_normed(2 * wave + part, 1).start()

    def pass_normed(u):
        for side in range(2):
            own_normed(u, side).wait_recv()
            onward_normed(u, side).start()

    for c in over_x2:
        c.wait_recv()
    share.start()
    pass_normed(0)
    own_out.wait()
    share.wait_recv()

    def place(u):
        wave = u // 2
        return wave, slice(u % 2 * many, (u % 2 + 1) * many), slice(wave * 256, (wave + 1) * 256)

    for u in range(4):
        if u > 0:
            pass_normed(u)
        wave, rows, depth = place(u)
        product = dot(ng[y, wave, rows, :], wown[depth, :])
        product = product + dot(ng[left, wave, rows, :], wop[0, depth, :])
        product = product + dot(ng[right, wave, rows, :], wop[1, depth, :])
        pacc[wave, rows, :] = product
    for u in range(4):
        onward_normed(u, 0).wait_recv()
        onward_normed(u, 1).wait_recv()
        wave, rows, depth = place(u)
        product = pacc[wave, rows, :] + dot(ng[across, wave, rows, :], wop[2, depth, :])
        if wave == 0:
            pacc[0, rows, :] = product
        else:
            out_ref[rows, :] = (pacc[0, rows, :] + product).astype(BF16)

    for r in range(BLOCKS):
        for side in range(2):
            own_rows(r, side).wait_send()
            onward(r, side).wait_send()
            own_normed(r, side).wait_send()
            onward_normed(r, side).wait_send()
    for c in decay_copies + fetch + over_z + over_x + over_x2 + [share]:
        c.wait_send()
    for wave in range(2):
        corner(wave, True).wait_send()
        corner(wave, False).wait_send()
        for bit in range(last_bit):
            if bit != 2:
                state_copy(bit, wave).wait_send()
            if bit > 0:
                hand_over(bit, wave).wait_send()

        @pl.when(is_source)
        def _(wave=wave):
            top_copy(wave, near, 0).wait_send()
            top_copy(wave, far, 1).wait_send()

        @pl.when(is_top)
        def _(wave=wave):
            hand_over(last_bit, wave).wait_send()


def body(tokens, log_decay, w_query, w_key, w_value, w_level, w_out):
    hbm = pl.BlockSpec(memory_space=pl.ANY)
    vmem = pl.BlockSpec(memory_space=pltpu.VMEM)
    dma = pltpu.SemaphoreType.DMA
    wide = HEADS * LEVELS
    return pl.pallas_call(
        kernel,
        name="layer",
        out_shape=pltpu.VMEM((ROWS, PART), BF16),
        in_specs=[hbm, vmem, hbm, hbm, hbm, vmem, hbm],
        out_specs=vmem,
        scratch_shapes=[
            pltpu.VMEM((4, ROWS, PART), BF16),
            pltpu.VMEM((4 * PART, HEADS * SIZE), BF16),
            pltpu.VMEM((4 * PART, 2 * SIZE), BF16),
            pltpu.VMEM((HEADS * SIZE, PART), BF16),
            pltpu.VMEM((3, HEADS * SIZE, PART), BF16),
            pltpu.VMEM((4, 2, ROWS, 2 * SIZE), BF16),
            pltpu.VMEM((2, ROWS, PART), F32),
            pltpu.VMEM((SIZE, ROWS), F32),
            pltpu.VMEM((ROWS, wide), F32),
            pltpu.VMEM((8, ROWS), F32),
            pltpu.VMEM((BLOCKS, 8, SIZE), F32),
            pltpu.VMEM((8, wide), F32),
            pltpu.VMEM((BITS - 1, 24, SIZE), F32),
            pltpu.VMEM((BITS - 1, 24, SIZE), F32),
            pltpu.VMEM((BITS - 1, 2, 8, SIZE), F32),
            pltpu.VMEM((2, 8, SIZE), F32),
            pltpu.VMEM((2, HEADS * SIZE, SIZE), BF16),
            pltpu.VMEM((ROWS, HEADS * SIZE), BF16),
            pltpu.VMEM((ROWS, SIZE), BF16),
            pltpu.VMEM((ROWS, SIZE), BF16),
            pltpu.VMEM((ROWS, HEADS * SIZE), F32),
            pltpu.VMEM((BITS, ROWS, HEADS * SIZE), BF16),
            pltpu.VMEM((BLOCKS, HEADS * SIZE, SIZE), F32),
            pltpu.VMEM((HEADS * SIZE, SIZE), BF16),
            pltpu.VMEM((HEADS * SIZE, SIZE), F32),
            pltpu.VMEM((BITS, HEADS * SIZE, SIZE), BF16),
            pltpu.VMEM((BITS, HEADS * SIZE, SIZE), BF16),
            dma((4 * BLOCKS,)), dma((4 * BLOCKS,)),
            dma((BITS - 1,)), dma((BITS - 1,)),
            dma((2 * BITS + 2,)), dma((2 * BITS,)),
            dma((2,)), dma((2,)),
            dma((2 * BITS,)), dma((2 * BITS,)),
            dma((12,)), dma((12,)),
            dma((4 * BLOCKS,)), dma((4 * BLOCKS,)),
            dma((5,)),
        ],
        compiler_params=pltpu.CompilerParams(
            collective_id=0, has_side_effects=True, vmem_limit_bytes=56 << 20
        ),
        cost_estimate=pl.CostEstimate(flops=7_000_000_000, bytes_accessed=14_000_000, transcendentals=400_000),
    )(tokens, log_decay.T, w_query, w_key, w_value, w_level.T, w_out)


def solution(mesh):
    in_specs = (
        P("seq", "tp"),
        P("seq", "tp"),
        P(None, "tp"),
        P(None, "tp"),
        P(None, "tp"),
        P(None, "tp"),
        P("tp", None),
    )
    return jax.shard_map(
        body, mesh=mesh, in_specs=in_specs, out_specs=P("seq", "tp"), check_vma=False
    )
```

time: 94.2 us -> 85 us (0.902)
  Pallas kernels: 93.1 us -> 83.9 us
    pallas_call x1, Pallas kernels: 93.1 us -> 83.9 us  [body(): pl.pallas_call(kernel, name='layer', out_shape=pltpu.VMEM((ROWS, PART), B...]
where the time goes in v3:
time: 85 us; the launch traced here: 84.9 us
  Pallas kernels  83.9 us (99%)
  local copies, waits for them, and re-layouts  0.97 us (1%)
    pallas_call x1, Pallas kernels, body(): pl.pallas_call(kernel, name='layer', out_shape=pltpu.VMEM((ROWS, PART), B...  83.9 us

profile of v3, /device:TPU:1, one launch (start us, length us, event | category | flops | bytes accessed | tf_op | source)
XLA Modules:
  0.0 84.9 jit_solution(14072774163644188502)
XLA Ops:
  0.0 83.9 %layer.1 = bf16[512,1024]{1,0:T(8,128)(2,1)S(1)} custom-call(bf16[512,1024]{1,0:T(8,128)(2,1)} %x_ref.1, f32[4,512]{1,0:T(4,128)} %bitcast.3, bf16[4096,512]{1,0:T(8,128)(2,1)} %wq_ref.1, bf16[4096,128]{1,0:T(8,128)(2,1)} %wk_ref.1, bf16[4096,128]{1,0:T(8,128)(2,1)} %wv_ref.1, bf16[36,4096]{1,0:T(8,128)(2,1)} %bitcast.2, bf16[512,4096]{1,0:T(8,128)(2,1)} %wo_ref.1), custom_call_target="tpu_custom_call" | custom-call | flops 7000000000 | bytes 14000000 | tf_op jit(solution)/shard_map/layer/pallas_call | solution.py:526
  83.9 1.0 %copy.9 = bf16[512,1024]{1,0:T(8,128)(2,1)} copy(bf16[512,1024]{1,0:T(8,128)(2,1)S(1)} %layer.1) | data formatting | bytes 2097152

commit v4 on v3

--- a/solution.py
+++ b/solution.py
@@ -17,6 +17,8 @@
 BLOCKS = ROWS // BLOCK
 PART = 1024
 BITS = 6
+EARLY = 2
+LATE = ROWS - EARLY * BLOCK
 
 
 def dot(a, b):
@@ -41,10 +43,10 @@
 
 def kernel(
     x_ref, ld_ref, wq_ref, wk_ref, wv_ref, wl_ref, wo_ref, out_ref,
-    xg, wq, wkv, wown, wop, ng, pacc,
+    xg, wq, wkv, wkp, psend, prec, wown, wop, ng, pacc,
     ldp, d36, dect, ends, offs, gsend, grecv, coef, pair, xin,
     qb, kb, vb, acc, qs, sb, sb16, run, ssend, bkt,
-    tok_s, tok_r, dec_s, dec_r, st_s, st_r, xs, xr, fw_s, fw_r, wo_s, wo_r, nm_s, nm_r, loc,
+    tok_s, tok_r, dec_s, dec_r, st_s, st_r, xs, xr, fw_s, fw_r, wo_s, wo_r, kv_s, kv_r, nm_s, nm_r, loc,
 ):
     y = lax.axis_index("tp")
     s = lax.axis_index("seq")
@@ -145,7 +147,26 @@
         spread_copy(10, some_rows((3 - cx) * 8, 8), cols_b, mates[1]),
     ]
     share = spread_copy(11, pl.ds(0, ROWS), wide_cols, mates[0])
-    for c in fetch:
+
+    eighth = pl.ds(pl.multiple_of((core * 4 + cx) * 128, 128), 128)
+    core_rows = pl.ds(pl.multiple_of(core * 512, 512), 512)
+    kv_fetch = []
+    for i, (peer, device) in enumerate(((right, to_right), (left, to_left), (across, to_across))):
+        there = pl.ds(pl.multiple_of(peer * PART + (core * 4 + cx) * 128, 128), 128)
+        kv_fetch.append(remote(wkv.at[there], wkp.at[i, eighth], kv_s.at[i], kv_r.at[i], device))
+    kv_x = [
+        remote(wkp.at[:, eighth], wkp.at[:, eighth], kv_s.at[3 + i], kv_r.at[3 + i], device)
+        for i, device in enumerate((mates[1], mates[2], x_across))
+    ]
+    kv_share = remote(wkp.at[:, core_rows], wkp.at[:, core_rows], kv_s.at[6], kv_r.at[6], mates[0])
+    kv_parts = [
+        remote(psend.at[0], prec.at[1], kv_s.at[7], kv_r.at[7], to_left),
+        remote(psend.at[1], prec.at[0], kv_s.at[8], kv_r.at[8], to_right),
+        remote(psend.at[2], prec.at[2], kv_s.at[9], kv_r.at[9], to_across),
+    ]
+    locals_[1].wait()
+    locals_[2].wait()
+    for c in kv_fetch:
         c.start()
 
     half = BLOCK // 2
@@ -161,7 +182,7 @@
         owner = right if side else left
         return remote(xg.at[owner, rows], xg.at[owner, rows], tok_s.at[i], tok_r.at[i], to_left if side else to_right)
 
-    for r in range(3):
+    def send_own(r):
         own_rows(r, 0).start()
         own_rows(r, 1).start()
 
@@ -169,8 +190,6 @@
         for side in range(2):
             own_rows(r, side).wait_recv()
             onward(r, side).start()
-            if r + 3 < BLOCKS:
-                own_rows(r + 3, side).start()
 
     ldp[...] = jnp.zeros_like(ldp)
     ldp[0:HEADS, :] = ld_ref[...]
@@ -196,21 +215,27 @@
     gap_off = jnp.zeros((8, HEADS * LEVELS), F32)
     decay_copies = []
     for bit in range(BITS - 1):
-        if bit == 2:
-            for c in fetch:
-                c.wait_recv()
-            over_z[0].start()
-        if bit == 3:
-            over_z[0].wait_recv()
-            over_z[1].start()
-            pass_on(0)
-        if bit == 4:
-            over_z[1].wait_recv()
-            over_z[2].start()
-            pass_on(1)
         up = uppers[bit].astype(F32)
         c = remote(gsend.at[bit], grecv.at[bit], dec_s.at[bit], dec_r.at[bit], mates[bit])
         c.start()
+        if bit == 0:
+            send_own(0)
+            for d in fetch:
+                d.start()
+        if bit == 2:
+            send_own(1)
+            for d in kv_fetch:
+                d.wait_recv()
+            for d in kv_x:
+                d.start()
+            for d in fetch:
+                d.wait_recv()
+            over_z[0].start()
+        if bit == 3:
+            pass_on(0)
+        if bit == 4:
+            over_z[0].wait_recv()
+            over_z[1].start()
         c.wait_recv()
         decay_copies.append(c)
         mine = gsend[bit]
@@ -231,8 +256,12 @@
     up = uppers[BITS - 1].astype(F32)
     gap_off = gap_off + jnp.where(level_of == 3 + BITS - 1, up * before + (1.0 - up) * NEVER, 0.0)
     offs[...] = gap_off
-    for c in locals_:
+    for c in (locals_[0], locals_[3]):
         c.wait()
+    pass_on(1)
+    for c in kv_x:
+        c.wait_recv()
+    kv_share.start()
 
     owners = (y, left, right, across)
 
@@ -245,7 +274,17 @@
         part = project(r, wkv, owners[:3])
         onward(r, 0).wait_recv()
         onward(r, 1).wait_recv()
-        both = part + project(r, wkv, owners[3:])
+        finish_keys(r, part + project(r, wkv, owners[3:]))
+
+    def keys_late(r):
+        rows = pl.ds((r - EARLY) * BLOCK, BLOCK)
+        both = project(r, wkv, owners[:1])
+        for i in range(3):
+            both = both + prec[i, rows, :].astype(F32)
+        finish_keys(r, both)
+
+    def finish_keys(r, both):
+        rows = pl.ds(r * BLOCK, BLOCK)
         values = both[:, SIZE:].astype(BF16)
         kb[rows, :] = both[:, :SIZE].astype(BF16)
         vb[rows, :] = values
@@ -299,18 +338,23 @@
             cols = slice(h * SIZE, (h + 1) * SIZE)
             sb16[cols, :] = (sb[1, cols, :] + fade_of(1, 0, h) * sb[0, cols, :]).astype(BF16)
 
-    pass_on(2)
     keys_part(0)
-    over_z[2].wait_recv()
-    for c in over_x:
-        c.start()
-    query_part(0)
-    pass_on(3)
+    kv_share.wait_recv()
+    for i in (2, 0, 1):
+        psend[i] = dot(xg[y, EARLY * BLOCK :, :], wkp[i]).astype(BF16)
+        kv_parts[i].start()
+    over_z[1].wait_recv()
+    over_z[2].start()
     keys_part(1)
     pair_sum()
+    query_part(0)
     query_part(1)
-    keys_part(2)
-    keys_part(BLOCKS - 1)
+    send_own(2)
+    for c in kv_parts:
+        c.wait_recv()
+    send_own(3)
+    for r in range(EARLY, BLOCKS):
+        keys_late(r)
     for h in range(HEADS):
         cols = slice(h * SIZE, (h + 1) * SIZE)
         first = sb[1, cols, :] + fade_of(1, 0, h) * sb[0, cols, :]
@@ -370,7 +414,6 @@
         corner(wave, False).start()
         state_copy(1, wave).start()
         corner(wave, True).start()
-    query_part(2)
     for wave in range(2):
         one = head_rows(wave)
         state_copy(1, wave).wait_recv()
@@ -385,11 +428,10 @@
         bkt[2, one, :] = second.astype(BF16)
         hand_over(1, wave).start()
         hand_over(2, wave).start()
+    over_z[2].wait_recv()
     for c in over_x:
-        c.wait_recv()
-    for c in over_x2:
         c.start()
-    query_part(BLOCKS - 1)
+    pass_on(2)
     for wave in range(2):
         one = head_rows(wave)
         state_copy(3, wave).wait_recv()
@@ -398,10 +440,7 @@
         ssend[4, one, :] = merged.astype(BF16)
         state_copy(4, wave).start()
         hand_over(3, wave).start()
-    take(0)
-    for wave in range(2):
-        hand_over(1, wave).wait_recv()
-    take(1)
+    pass_on(3)
     for wave in range(2):
         one = head_rows(wave)
         state_copy(4, wave).wait_recv()
@@ -413,10 +452,14 @@
             top_copy(wave, far, 1).start()
 
         hand_over(4, wave).start()
-    for bit in (2, 3):
-        for wave in range(2):
-            hand_over(bit, wave).wait_recv()
-        take(bit)
+    for c in over_x:
+        c.wait_recv()
+    for c in over_x2:
+        c.start()
+    for r in range(2, BLOCKS):
+        onward(r, 0).wait_recv()
+        onward(r, 1).wait_recv()
+        query_part(r)
 
     many = ROWS // 2
 
@@ -437,9 +480,11 @@
             top_copy(wave, source, 0).wait_recv()
             hand_over(last_bit, wave).start()
 
-    for wave in range(2):
-        hand_over(last_bit - 1, wave).wait_recv()
-    take(last_bit - 1)
+    for bit in range(last_bit):
+        if bit > 0:
+            for wave in range(2):
+                hand_over(bit, wave).wait_recv()
+        take(bit)
     for wave in range(2):
 
         @pl.when(is_top)
@@ -462,10 +507,12 @@
             own_normed(u, side).wait_recv()
             onward_normed(u, side).start()
 
+    pass_normed(0)
     for c in over_x2:
         c.wait_recv()
     share.start()
-    pass_normed(0)
+    pass_normed(1)
+    pass_normed(2)
     own_out.wait()
     share.wait_recv()
 
@@ -474,8 +521,8 @@
         return wave, slice(u % 2 * many, (u % 2 + 1) * many), slice(wave * 256, (wave + 1) * 256)
 
     for u in range(4):
-        if u > 0:
-            pass_normed(u)
+        if u == 2:
+            pass_normed(3)
         wave, rows, depth = place(u)
         product = dot(ng[y, wave, rows, :], wown[depth, :])
         product = product + dot(ng[left, wave, rows, :], wop[0, depth, :])
@@ -497,7 +544,7 @@
             onward(r, side).wait_send()
             own_normed(r, side).wait_send()
             onward_normed(r, side).wait_send()
-    for c in decay_copies + fetch + over_z + over_x + over_x2 + [share]:
+    for c in decay_copies + kv_fetch + kv_x + [kv_share] + kv_parts + fetch + over_z + over_x + over_x2 + [share]:
         c.wait_send()
     for wave in range(2):
         corner(wave, True).wait_send()
@@ -533,6 +580,9 @@
             pltpu.VMEM((4, ROWS, PART), BF16),
             pltpu.VMEM((4 * PART, HEADS * SIZE), BF16),
             pltpu.VMEM((4 * PART, 2 * SIZE), BF16),
+            pltpu.VMEM((3, PART, 2 * SIZE), BF16),
+            pltpu.VMEM((3, LATE, 2 * SIZE), BF16),
+            pltpu.VMEM((3, LATE, 2 * SIZE), BF16),
             pltpu.VMEM((HEADS * SIZE, PART), BF16),
             pltpu.VMEM((3, HEADS * SIZE, PART), BF16),
             pltpu.VMEM((4, 2, ROWS, 2 * SIZE), BF16),
@@ -563,6 +613,7 @@
             dma((2,)), dma((2,)),
             dma((2 * BITS,)), dma((2 * BITS,)),
             dma((12,)), dma((12,)),
+            dma((10,)), dma((10,)),
             dma((4 * BLOCKS,)), dma((4 * BLOCKS,)),
             dma((5,)),
         ],

time: 85 us -> 84.4 us (level)
  no operation moved by 1% of the time
where the time goes in v4:
time: 84.4 us; the launch traced here: 84.3 us
  Pallas kernels  83.3 us (99%)
  local copies, waits for them, and re-layouts  0.97 us (1%)
    pallas_call x1, Pallas kernels, body(): pl.pallas_call(kernel, name='layer', out_shape=pltpu.VMEM((ROWS, PART), B...  83.3 us

profile of v4, /device:TPU:1, one launch (start us, length us, event | category | flops | bytes accessed | tf_op | source)
XLA Modules:
  0.0 84.3 jit_solution(11065698398935340159)
XLA Ops:
  0.0 83.3 %layer.1 = bf16[512,1024]{1,0:T(8,128)(2,1)S(1)} custom-call(bf16[512,1024]{1,0:T(8,128)(2,1)} %x_ref.1, f32[4,512]{1,0:T(4,128)} %bitcast.3, bf16[4096,512]{1,0:T(8,128)(2,1)} %wq_ref.1, bf16[4096,128]{1,0:T(8,128)(2,1)} %wk_ref.1, bf16[4096,128]{1,0:T(8,128)(2,1)} %wv_ref.1, bf16[36,4096]{1,0:T(8,128)(2,1)} %bitcast.2, bf16[512,4096]{1,0:T(8,128)(2,1)} %wo_ref.1), custom_call_target="tpu_custom_call" | custom-call | flops 7000000000 | bytes 14000000 | tf_op jit(solution)/shard_map/layer/pallas_call | solution.py:573
  83.3 1.0 %copy.9 = bf16[512,1024]{1,0:T(8,128)(2,1)} copy(bf16[512,1024]{1,0:T(8,128)(2,1)S(1)} %layer.1) | data formatting | bytes 2097152

commit v5 on v4

--- a/solution.py
+++ b/solution.py
@@ -46,7 +46,7 @@
     xg, wq, wkv, wkp, psend, prec, wown, wop, ng, pacc,
     ldp, d36, dect, ends, offs, gsend, grecv, coef, pair, xin,
     qb, kb, vb, acc, qs, sb, sb16, run, ssend, bkt,
-    tok_s, tok_r, dec_s, dec_r, st_s, st_r, xs, xr, fw_s, fw_r, wo_s, wo_r, kv_s, kv_r, nm_s, nm_r, loc,
+    tok_s, tok_r, dec_s, dec_r, st_s, st_r, xs, xr, fw_s, fw_r, wo_s, wo_r, kv_s, kv_r, nm_s, nm_r, ready, loc,
 ):
     y = lax.axis_index("tp")
     s = lax.axis_index("seq")
@@ -93,27 +93,25 @@
         bkt[BITS - 1] = jnp.zeros((HEADS * SIZE, SIZE), BF16)
 
     barrier = pltpu.get_barrier_semaphore()
-    for peer in [to_right, to_left, to_across, opposite, x_across] + mates:
+    in_half = [to_right, to_left, to_across, x_across] + mates
+    for peer in in_half:
         pl.semaphore_signal(barrier, inc=1, device_id=peer, device_id_type=MESH)
+
+    @pl.when(jnp.logical_not(is_top))
+    def _():
+        pl.semaphore_signal(barrier, inc=1, device_id=opposite, device_id_type=MESH)
+
+    @pl.when(is_source)
+    def _():
+        pl.semaphore_signal(barrier, inc=1, device_id=near, device_id_type=MESH)
+        pl.semaphore_signal(barrier, inc=1, device_id=far, device_id_type=MESH)
+
+    pl.semaphore_wait(barrier, len(in_half) + jnp.where(is_top, 2, 0))
 
     @pl.when(is_top)
     def _():
-        pl.semaphore_signal(barrier, inc=1, device_id=source, device_id_type=MESH)
-
-    pl.semaphore_wait(barrier, 5 + len(mates) + jnp.where(is_source, 2, 0))
-
-    half = BLOCK // 2
-
-    def own_rows(r, side):
-        rows = pl.ds(pl.multiple_of(r * BLOCK, BLOCK), BLOCK)
-        i = 2 * r + side
-        return remote(x_ref.at[rows], xg.at[y, rows], tok_s.at[i], tok_r.at[i], to_left if side else to_right)
-
-    def onward(r, side):
-        rows = pl.ds(pl.multiple_of(r * BLOCK + side * half, half), half)
-        i = 2 * BLOCKS + 2 * r + side
-        owner = right if side else left
-        return remote(xg.at[owner, rows], xg.at[owner, rows], tok_s.at[i], tok_r.at[i], to_left if side else to_right)
+        pl.semaphore_signal(ready.at[0], inc=1, device_id=opposite, device_id_type=MESH)
+        pl.semaphore_signal(ready.at[1], inc=1, device_id=source, device_id_type=MESH)
 
     wide_cols = pl.ds(pl.multiple_of(core * 512, 512), 512)
     cols_a = pl.ds(pl.multiple_of(core * 512, 256), 256)
@@ -344,6 +342,11 @@
         psend[i] = dot(xg[y, EARLY * BLOCK :, :], wkp[i]).astype(BF16)
         kv_parts[i].start()
     over_z[1].wait_recv()
+
+    @pl.when(jnp.logical_not(is_top))
+    def _():
+        pl.semaphore_wait(ready.at[0], 1)
+
     over_z[2].start()
     keys_part(1)
     pair_sum()
@@ -448,6 +451,8 @@
 
         @pl.when(is_source)
         def _(wave=wave):
+            if wave == 0:
+                pl.semaphore_wait(ready.at[1], 2)
             top_copy(wave, near, 0).start()
             top_copy(wave, far, 1).start()
 
@@ -615,7 +620,7 @@
             dma((12,)), dma((12,)),
             dma((10,)), dma((10,)),
             dma((4 * BLOCKS,)), dma((4 * BLOCKS,)),
-            dma((5,)),
+            pltpu.SemaphoreType.REGULAR((2,)), dma((5,)),
         ],
         compiler_params=pltpu.CompilerParams(
             collective_id=0, has_side_effects=True, vmem_limit_bytes=56 << 20

time: 84.4 us -> 81.1 us (0.961)
  Pallas kernels: 83.3 us -> 80 us
    pallas_call x1, Pallas kernels: 83.3 us -> 80 us  [body(): pl.pallas_call(kernel, name='layer', out_shape=pltpu.VMEM((ROWS, PART), B...]
where the time goes in v5:
time: 81.1 us; the launch traced here: 81 us
  Pallas kernels  80 us (99%)
  local copies, waits for them, and re-layouts  0.97 us (1%)
    pallas_call x1, Pallas kernels, body(): pl.pallas_call(kernel, name='layer', out_shape=pltpu.VMEM((ROWS, PART), B...  80 us

profile of v5, /device:TPU:1, one launch (start us, length us, event | category | flops | bytes accessed | tf_op | source)
XLA Modules:
  0.0 81.0 jit_solution(14896059650126687352)
XLA Ops:
  0.0 80.0 %layer.1 = bf16[512,1024]{1,0:T(8,128)(2,1)S(1)} custom-call(bf16[512,1024]{1,0:T(8,128)(2,1)} %x_ref.1, f32[4,512]{1,0:T(4,128)} %bitcast.3, bf16[4096,512]{1,0:T(8,128)(2,1)} %wq_ref.1, bf16[4096,128]{1,0:T(8,128)(2,1)} %wk_ref.1, bf16[4096,128]{1,0:T(8,128)(2,1)} %wv_ref.1, bf16[36,4096]{1,0:T(8,128)(2,1)} %bitcast.2, bf16[512,4096]{1,0:T(8,128)(2,1)} %wo_ref.1), custom_call_target="tpu_custom_call" | custom-call | flops 7000000000 | bytes 14000000 | tf_op jit(solution)/shard_map/layer/pallas_call | solution.py:578
  80.0 1.0 %copy.9 = bf16[512,1024]{1,0:T(8,128)(2,1)} copy(bf16[512,1024]{1,0:T(8,128)(2,1)S(1)} %layer.1) | data formatting | bytes 2097152

commit v6 on v5

--- a/solution.py
+++ b/solution.py
@@ -234,6 +234,10 @@
         if bit == 4:
             over_z[0].wait_recv()
             over_z[1].start()
+            pass_on(1)
+            for d in kv_x:
+                d.wait_recv()
+            kv_share.start()
         c.wait_recv()
         decay_copies.append(c)
         mine = gsend[bit]
@@ -256,10 +260,6 @@
     offs[...] = gap_off
     for c in (locals_[0], locals_[3]):
         c.wait()
-    pass_on(1)
-    for c in kv_x:
-        c.wait_recv()
-    kv_share.start()
 
     owners = (y, left, right, across)
 

time: 81.1 us -> 77.9 us (0.961)
  Pallas kernels: 80 us -> 76.8 us
    pallas_call x1, Pallas kernels: 80 us -> 76.8 us  [body(): pl.pallas_call(kernel, name='layer', out_shape=pltpu.VMEM((ROWS, PART), B...]
where the time goes in v6:
time: 77.9 us; the launch traced here: 77.8 us
  Pallas kernels  76.8 us (99%)
  local copies, waits for them, and re-layouts  0.97 us (1%)
    pallas_call x1, Pallas kernels, body(): pl.pallas_call(kernel, name='layer', out_shape=pltpu.VMEM((ROWS, PART), B...  76.8 us

profile of v6, /device:TPU:1, one launch (start us, length us, event | category | flops | bytes accessed | tf_op | source)
XLA Modules:
  0.0 77.8 jit_solution(15639172434971191551)
XLA Ops:
  0.0 76.8 %layer.1 = bf16[512,1024]{1,0:T(8,128)(2,1)S(1)} custom-call(bf16[512,1024]{1,0:T(8,128)(2,1)} %x_ref.1, f32[4,512]{1,0:T(4,128)} %bitcast.3, bf16[4096,512]{1,0:T(8,128)(2,1)} %wq_ref.1, bf16[4096,128]{1,0:T(8,128)(2,1)} %wk_ref.1, bf16[4096,128]{1,0:T(8,128)(2,1)} %wv_ref.1, bf16[36,4096]{1,0:T(8,128)(2,1)} %bitcast.2, bf16[512,4096]{1,0:T(8,128)(2,1)} %wo_ref.1), custom_call_target="tpu_custom_call" | custom-call | flops 7000000000 | bytes 14000000 | tf_op jit(solution)/shard_map/layer/pallas_call | solution.py:578
  76.8 1.0 %copy.9 = bf16[512,1024]{1,0:T(8,128)(2,1)} copy(bf16[512,1024]{1,0:T(8,128)(2,1)S(1)} %layer.1) | data formatting | bytes 2097152

commit v7 on v6

--- a/solution.py
+++ b/solution.py
@@ -220,8 +220,9 @@
             send_own(0)
             for d in fetch:
                 d.start()
+        if bit == 1:
+            send_own(1)
         if bit == 2:
-            send_own(1)
             for d in kv_fetch:
                 d.wait_recv()
             for d in kv_x:

time: 77.9 us -> 77.9 us (level)
  no operation moved by 1% of the time
where the time goes in v7:
time: 77.9 us; the launch traced here: 77.8 us
  Pallas kernels  76.8 us (99%)
  local copies, waits for them, and re-layouts  0.97 us (1%)
    pallas_call x1, Pallas kernels, body(): pl.pallas_call(kernel, name='layer', out_shape=pltpu.VMEM((ROWS, PART), B...  76.8 us

profile of v7, /device:TPU:1, one launch (start us, length us, event | category | flops | bytes accessed | tf_op | source)
XLA Modules:
  0.0 77.8 jit_solution(4534907036191788949)
XLA Ops:
  0.0 76.8 %layer.1 = bf16[512,1024]{1,0:T(8,128)(2,1)S(1)} custom-call(bf16[512,1024]{1,0:T(8,128)(2,1)} %x_ref.1, f32[4,512]{1,0:T(4,128)} %bitcast.3, bf16[4096,512]{1,0:T(8,128)(2,1)} %wq_ref.1, bf16[4096,128]{1,0:T(8,128)(2,1)} %wk_ref.1, bf16[4096,128]{1,0:T(8,128)(2,1)} %wv_ref.1, bf16[36,4096]{1,0:T(8,128)(2,1)} %bitcast.2, bf16[512,4096]{1,0:T(8,128)(2,1)} %wo_ref.1), custom_call_target="tpu_custom_call" | custom-call | flops 7000000000 | bytes 14000000 | tf_op jit(solution)/shard_map/layer/pallas_call | solution.py:579
  76.8 1.0 %copy.9 = bf16[512,1024]{1,0:T(8,128)(2,1)} copy(bf16[512,1024]{1,0:T(8,128)(2,1)S(1)} %layer.1) | data formatting | bytes 2097152
